TPU v7x, 256 devices: a whole 4x4x8 slice. The times are simulated.
256 devices in a mesh: table: 64 (over y, z, core), dp: 4 (over x).
Axes of the slice: x: 4, y: 4, z: 8, core: 2. Of those that a mesh axis runs over, the one named last changes fastest.
Arguments:
- owners: int32 [131072, 8], P(('table', 'dp')), may hold values from 0 to 63, all different within a row; in each aligned block of 512 rows (0 to 511, 512 to 1023, ...) at most 128 rows name the same one
- local_rows: int32 [131072, 8], P(('table', 'dp')), may hold values from 0 to 4095
- grad_pooled: bfloat16 [131072, 128], P(('table', 'dp')), may hold values from -4 to 4
- table: float32 [262144, 128], P('table'), may hold values from -6 to 6
- accum: float32 [262144], P('table'), may hold values from 0.1 to 4
- parity: float32 [8192, 128], P('table'), may hold values from -6 to 6
- parity_slot: int32 [262144], P('table'), may hold values from 0 to 8191, as said below
Outputs:
- pooled: bfloat16 [131072, 128], P(('table', 'dp'))
- new_table: float32 [262144, 128], P('table')
- new_accum: float32 [262144], P('table')
- new_parity: float32 [8192, 128], P('table')
Inputs may be any that keep to these rules, and one draw needn't show every extreme that they name: `owners`: each bag names 8 different table devices. Among the 512 bags of one device (aligned blocks of rows), no table device is named by more than 128 bags, and in some blocks one is named by exactly 128. `parity_slot`: within the 4096 rows of one table device the values are distinct, and each device's rows include the value 8192 - 1. Parity row v is held by the table device v // 128.
All inputs are finite; a program needn't handle non-finite values.
Results may differ from a plain program's by a relative error of at most 0.0085.
Values may be sent and summed in bfloat16 or wider, within the bound.
A program may use at most 64 MiB of HBM per device.

v0:
```python
import jax
import jax.numpy as jnp
from jax import lax
from jax.sharding import PartitionSpec as P

LEARN = 0.5
EPSILON = 1e-06


def adagrad(old_rows, old_accum, row_grads):
    fresh_accum = old_accum + jnp.mean(row_grads * row_grads, axis=1)
    fresh_rows = old_rows - LEARN * row_grads / jnp.sqrt(fresh_accum + EPSILON)[:, None]
    return (fresh_rows, fresh_accum)


def fold_sources(received):
    return jnp.sum(received, axis=0)


def on_device(owners, local_rows, grad_pooled, table, accum, parity, parity_slot):
    table_count = lax.axis_size("table")
    bag_count, per_bag = owners.shape
    row_count, row_width = table.shape
    lookup_count = bag_count * per_bag
    capacity = min(bag_count, 2 * lookup_count // table_count)
    slot_count = table_count * capacity
    owner_flat = owners.reshape(lookup_count)
    local_flat = local_rows.reshape(lookup_count)
    owner_hits = (owner_flat[:, None] == jnp.arange(table_count, dtype=jnp.int32)[None, :]).astype(
        jnp.int32
    )
    slot_rank = jnp.sum((jnp.cumsum(owner_hits, axis=0) - 1) * owner_hits, axis=1)
    position = owner_flat * capacity + slot_rank
    requests = jnp.full((slot_count,), row_count, jnp.int32).at[position].set(local_flat)
    requests = requests.reshape(table_count, capacity)
    table_half = table.astype(jnp.bfloat16)
    asked_rows = lax.all_to_all(requests, "table", split_axis=0, concat_axis=0, tiled=True)
    fetched = jnp.take(table_half, jnp.minimum(asked_rows, row_count - 1), axis=0)
    returned = lax.all_to_all(fetched, "table", split_axis=0, concat_axis=0, tiled=True)
    returned_rows, asked_rows = (returned, asked_rows)
    gathered = returned_rows.reshape(slot_count, row_width)[position]
    pooled = jnp.sum(
        gathered.reshape(bag_count, per_bag, row_width).astype(jnp.float32), axis=1
    ).astype(jnp.bfloat16)
    spread = jnp.repeat(grad_pooled, per_bag, axis=0)
    outgoing = jnp.zeros((slot_count, row_width), jnp.bfloat16).at[position].set(spread)
    incoming = lax.all_to_all(
        outgoing.reshape(table_count, capacity, row_width),
        "table",
        split_axis=0,
        concat_axis=0,
        tiled=True,
    )
    row_ids = jnp.minimum(asked_rows, row_count - 1).reshape(slot_count)
    partial_grads = jax.ops.segment_sum(
        incoming.reshape(slot_count, row_width).astype(jnp.float32), row_ids, num_segments=row_count
    )
    row_grads = lax.psum(partial_grads.astype(jnp.bfloat16), "dp").astype(jnp.float32)
    new_table, new_accum = adagrad(table, accum, row_grads)
    row_delta = new_table - table
    parity_count = parity.shape[0]
    buffer = (
        jnp.zeros((table_count * parity_count, row_width), jnp.float32)
        .at[parity_slot]
        .set(row_delta)
    )
    buffer = buffer.reshape(table_count, parity_count, row_width)
    parity_sum = fold_sources(
        lax.all_to_all(
            buffer.astype(jnp.bfloat16), "table", split_axis=0, concat_axis=0, tiled=True
        ).astype(buffer.dtype)
    )
    new_parity = parity + parity_sum
    return (pooled, new_table, new_accum, new_parity)


def solution(mesh):
    in_specs = (
        P(("table", "dp"), None),
        P(("table", "dp"), None),
        P(("table", "dp"), None),
        P("table", None),
        P("table"),
        P("table", None),
        P("table"),
    )
    out_specs = (P(("table", "dp"), None), P("table", None), P("table"), P("table", None))
    return jax.shard_map(
        on_device, mesh=mesh, in_specs=in_specs, out_specs=out_specs, check_vma=False
    )
```

profile of v0, /device:TPU:32, one launch (start us, length us, event | category | flops | bytes accessed | tf_op | source)
XLA Modules:
  0.0 395.0 jit_solution(6233463178057744177)
XLA Ops:
  7.2 0.0 copy-start
  7.2 0.8 broadcast_multiply_fusion
  7.9 0.8 copy.18
  8.8 0.1 eq.29
  8.9 0.1 eq.25
  9.1 0.1 copy.17
  9.2 0.2 mul.30
  9.4 0.8 copy.22
  10.2 0.1 reshape.149
  10.4 0.1 fusion.14
  10.5 18.4 %reduce-window.6 = s32[64,32,128]{2,1,0:T(8,128)S(1)} reduce-window(s32[64,32,128]{2,1,0:T(8,128)S(1)} %fusion.14, s32[]{:T(128)} %constant.14.clone.1), window={size=1x1x128 pad=0_0x0_0x127_0}, to_apply=%region_0.0 | reduce-window | flops 33292288 | bytes 2097156 | tf_op jit(solution)/shard_map/reduce-window
  29.0 0.3 slice.12
  29.3 0.4 copy.23
  29.7 0.2 reduce-window.9
  29.9 0.3 add_add_fusion
  30.3 0.8 fusion.9
  31.1 16.1 %scatter_custom_fusion = s32[8192]{0:T(1024)} fusion(s32[4096]{0:T(1024)S(1)} %bitcast.51, s32[4096]{0:T(1024)S(1)} %reshape.149, s32[]{:T(128)} %constant.12.clone.1), kind=kCustom, calls=%fused_computation.41 | custom fusion | bytes 32772 | tf_op jit(solution)/shard_map/scatter | solution.py:34
  47.2 11.8 %all-to-all-start = ((s32[64,1,128]{2,1,0:T(1,128)}), s32[64,1,128]{2,1,0:T(1,128)S(1)}, u32[]{:S(2)}, u32[]{:S(2)}) async-start(s32[64,1,128]{2,1,0:T(1,128)} %bitcast.5), calls=%async_computation | async-start | bytes 65536 | tf_op jit(solution)/shard_map/all_to_all | solution.py:37
  59.0 0.0 copy-done
  59.0 12.4 %scatter_custom_fusion.1 = bf16[8192,128]{1,0:T(8,128)(2,1)} fusion(s32[4096]{0:T(1024)S(1)} %bitcast.52, bf16[]{:T(256)} %constant.20.clone.1, bf16[512,128]{1,0:T(8,128)(2,1)S(1)} %copy-done), kind=kCustom, calls=%fused_computation.21 | custom fusion | bytes 2228226 | tf_op jit(solution)/shard_map/scatter | solution.py:46
  71.4 0.0 all-to-all-done
  71.4 10.3 %all-to-all-start.2 = ((bf16[64,128,128]{2,1,0:T(8,128)(2,1)}), bf16[64,128,128]{2,1,0:T(8,128)(2,1)S(1)}, u32[]{:S(2)}, u32[]{:S(2)}) async-start(bf16[64,128,128]{2,1,0:T(8,128)(2,1)} %bitcast.14), calls=%async_computation.2 | async-start | bytes 4194304 | tf_op jit(solution)/shard_map/all_to_all | solution.py:47
  81.7 0.0 all-reduce.2.cloned.1.call-start
  81.8 49.7 %all-to-all-done.2 = bf16[64,128,128]{2,1,0:T(8,128)(2,1)S(1)} async-done(((bf16[64,128,128]{2,1,0:T(8,128)(2,1)}), bf16[64,128,128]{2,1,0:T(8,128)(2,1)S(1)}, u32[]{:S(2)}, u32[]{:S(2)}) %all-to-all-start.2) | async-done | bytes 2097184 | tf_op jit(solution)/shard_map/all_to_all | solution.py:47
  131.5 52.6 %scatter_custom_fusion.2 = f32[4096,128]{1,0:T(8,128)} fusion(s32[8192]{0:T(1024)S(1)} %bitcast.45, bf16[8192,128]{1,0:T(8,128)(2,1)S(1)} %bitcast.43, f32[]{:T(128)} %constant.21.clone.1), kind=kCustom, calls=%fused_computation.6 | custom fusion | flops 2097152 | bytes 4194308 | tf_op jit(solution)/shard_map/scatter-add | solution.py:55
  184.1 2.9 convert_element_type.35
  187.0 0.0 all-reduce.2.cloned.1.call-update
  187.1 48.9 %all-reduce.2.cloned.1.call-done = bf16[4096,128]{1,0:T(8,128)(2,1)} async-done(((bf16[4096,128]{1,0:T(8,128)(2,1)}), bf16[4096,128]{1,0:T(8,128)(2,1)}) %all-reduce.2.cloned.1.call-update) | async-done | bytes 1048592 | tf_op jit(solution)/shard_map/psum | solution.py:58
  236.0 1.8 fusion.4
  237.9 0.0 copy-done.4
  237.9 0.6 add_sqrt_fusion
  238.5 0.0 copy-done.1
  238.5 2.8 fusion.3
  241.3 24.0 %gather_fusion = bf16[8192,128]{1,0:T(8,128)(2,1)S(1)} fusion(bf16[4096,128]{1,0:T(8,128)(2,1)S(1)} %get-tuple-element.7, s32[8192]{0:T(1024)S(1)} %fusion.17), kind=kCustom, calls=%fused_computation | custom fusion | bytes 4227072 | tf_op jit(solution)/shard_map/jit(_take)/gather | solution.py:38
  265.3 2.7 broadcast_select_fusion
  268.0 10.6 %all-to-all-start.1 = ((bf16[64,128,128]{2,1,0:T(8,128)(2,1)}), bf16[64,128,128]{2,1,0:T(8,128)(2,1)S(1)}, u32[]{:S(2)}, u32[]{:S(2)}) async-start(bf16[64,128,128]{2,1,0:T(8,128)(2,1)} %broadcast_select_fusion), calls=%async_computation.1 | async-start | bytes 4194304 | tf_op jit(solution)/shard_map/all_to_all | solution.py:39
  278.6 0.0 copy-done.3
  278.6 13.4 %scatter_custom_fusion.3 = f32[8192,128]{1,0:T(8,128)} fusion(s32[4096]{0:T(1024)S(1)} %compare_select_fusion.3, f32[4096,128]{1,0:T(8,128)} %get-tuple-element.6, f32[4096,128]{1,0:T(8,128)} %param.10, f32[]{:T(128)} %constant.21.clone.1), kind=kCustom, calls=%fused_computation.14 | custom fusion | flops 524288 | bytes 8388612 | tf_op jit(solution)/shard_map/scatter | solution.py:65
  292.0 3.7 convert_element_type.37
  295.7 32.7 %all-to-all-done.1 = bf16[64,128,128]{2,1,0:T(8,128)(2,1)S(1)} async-done(((bf16[64,128,128]{2,1,0:T(8,128)(2,1)}), bf16[64,128,128]{2,1,0:T(8,128)(2,1)S(1)}, u32[]{:S(2)}, u32[]{:S(2)}) %all-to-all-start.1) | async-done | bytes 2097184 | tf_op jit(solution)/shard_map/all_to_all | solution.py:39
  328.4 7.5 %all-to-all-start.3 = ((bf16[64,128,128]{2,1,0:T(8,128)(2,1)}), bf16[64,128,128]{2,1,0:T(8,128)(2,1)}, u32[]{:S(2)}, u32[]{:S(2)}) async-start(bf16[64,128,128]{2,1,0:T(8,128)(2,1)} %bitcast.41), calls=%async_computation.3 | async-start | bytes 4194304 | tf_op jit(solution)/shard_map/all_to_all | solution.py:69
  335.9 12.1 %gather_fusion.1 = bf16[4096,128]{1,0:T(8,128)(2,1)S(1)} fusion(bf16[8192,128]{1,0:T(8,128)(2,1)S(1)} %bitcast.40, s32[4096]{0:T(1024)S(1)} %broadcast_clamp_fusion), kind=kCustom, calls=%fused_computation.1 | custom fusion | bytes 2113536 | tf_op jit(solution)/shard_map/gather | solution.py:41
  348.0 0.0 copy-start.2
  348.0 1.3 bitcast_reduce_fusion
  349.4 36.2 %all-to-all-done.3 = bf16[64,128,128]{2,1,0:T(8,128)(2,1)} async-done(((bf16[64,128,128]{2,1,0:T(8,128)(2,1)}), bf16[64,128,128]{2,1,0:T(8,128)(2,1)}, u32[]{:S(2)}, u32[]{:S(2)}) %all-to-all-start.3) | async-done | bytes 2097184 | tf_op jit(solution)/shard_map/all_to_all | solution.py:69
  385.6 1.9 convert_reduce_fusion
  387.5 0.0 copy-done.2
  387.5 0.6 add.75
  (9 shorter events, 0.1 us)
Async XLA Ops:
  7.2 51.9 %copy-start = (bf16[512,128]{1,0:T(8,128)(2,1)S(1)}, bf16[512,128]{1,0:T(8,128)(2,1)}, u32[]{:S(2)}) copy-start(bf16[512,128]{1,0:T(8,128)(2,1)} %param.9) | copy-start | bytes 393220
  47.2 24.2 %all-to-all-start = ((s32[64,1,128]{2,1,0:T(1,128)}), s32[64,1,128]{2,1,0:T(1,128)S(1)}, u32[]{:S(2)}, u32[]{:S(2)}) async-start(s32[64,1,128]{2,1,0:T(1,128)} %bitcast.5), calls=%async_computation | async-start | bytes 65536 | tf_op jit(solution)/shard_map/all_to_all | solution.py:37
  71.4 60.1 %all-to-all-start.2 = ((bf16[64,128,128]{2,1,0:T(8,128)(2,1)}), bf16[64,128,128]{2,1,0:T(8,128)(2,1)S(1)}, u32[]{:S(2)}, u32[]{:S(2)}) async-start(bf16[64,128,128]{2,1,0:T(8,128)(2,1)} %bitcast.14), calls=%async_computation.2 | async-start | bytes 4194304 | tf_op jit(solution)/shard_map/all_to_all | solution.py:47
  81.7 154.3 %all-reduce.2.cloned.1.call-start = ((), (), s32[]{:S(2)}) async-start(), calls=%async_computation.4 | async-start | bytes 2097152 | tf_op jit(solution)/shard_map/psum | solution.py:58
  184.1 53.7 %copy-start.4 = (f32[4096]{0:T(1024)S(1)}, f32[4096]{0:T(1024)}, u32[]{:S(2)}) copy-start(f32[4096]{0:T(1024)} %param.11) | copy-start | bytes 49156
  184.1 54.3 %copy-start.1 = (f32[4096,128]{1,0:T(8,128)S(1)}, f32[4096,128]{1,0:T(8,128)}, u32[]{:S(2)}) copy-start(f32[4096,128]{1,0:T(8,128)} %param.10) | copy-start | bytes 6291460
  268.0 10.6 %copy-start.3 = (s32[4096]{0:T(1024)S(1)}, s32[4096]{0:T(1024)}, u32[]{:S(2)}) copy-start(s32[4096]{0:T(1024)} %param.13) | copy-start | bytes 49156
  268.0 60.4 %all-to-all-start.1 = ((bf16[64,128,128]{2,1,0:T(8,128)(2,1)}), bf16[64,128,128]{2,1,0:T(8,128)(2,1)S(1)}, u32[]{:S(2)}, u32[]{:S(2)}) async-start(bf16[64,128,128]{2,1,0:T(8,128)(2,1)} %broadcast_select_fusion), calls=%async_computation.1 | async-start | bytes 4194304 | tf_op jit(solution)/shard_map/all_to_all | solution.py:39
  328.4 57.2 %all-to-all-start.3 = ((bf16[64,128,128]{2,1,0:T(8,128)(2,1)}), bf16[64,128,128]{2,1,0:T(8,128)(2,1)}, u32[]{:S(2)}, u32[]{:S(2)}) async-start(bf16[64,128,128]{2,1,0:T(8,128)(2,1)} %bitcast.41), calls=%async_computation.3 | async-start | bytes 4194304 | tf_op jit(solution)/shard_map/all_to_all | solution.py:69
  348.0 39.5 %copy-start.2 = (f32[128,128]{1,0:T(8,128)S(1)}, f32[128,128]{1,0:T(8,128)}, u32[]{:S(2)}) copy-start(f32[128,128]{1,0:T(8,128)} %param.12) | copy-start | bytes 196612
Sparse Core Ops, SparseCore 0:
  187.2 48.8 all-reduce.1
where the time goes:
time: 399 us; the launch traced here: 395 us
  waiting for transfers between devices  168 us (42%)
  other arithmetic  105 us (26%)
  local copies, waits for them, and re-layouts  67.9 us (17%)
  starting transfers between devices  40.2 us (10%)
  between operations  14.2 us (4%)
    scatter-add x1, other arithmetic, on_device(): jax.ops.segment_sum(incoming.reshape(slot_count, row_width).astype(jnp.fl...  52.6 us
    all_to_all x1, waiting for transfers between devices, on_device(): lax.all_to_all(outgoing.reshape(table_count, capacity, row_width), 'table...  49.7 us
    psum x1, waiting for transfers between devices, on_device(): lax.psum(partial_grads.astype(jnp.bfloat16), 'dp').astype(jnp.float32)  48.9 us
    all_to_all x1, waiting for transfers between devices, on_device(): lax.all_to_all(buffer.astype(jnp.bfloat16), 'table', split_axis=0, concat...  36.2 us
    all_to_all x1, waiting for transfers between devices, on_device(): lax.all_to_all(fetched, 'table', split_axis=0, concat_axis=0, tiled=True)  32.7 us
    gather x1, local copies, waits for them, and re-layouts, on_device(): jnp.take(table_half, jnp.minimum(asked_rows, row_count - 1), axis=0)  24 us
    another operation x2, other arithmetic  18.6 us
    scatter x1, local copies, waits for them, and re-layouts, on_device(): jnp.full((slot_count,), row_count, jnp.int32).at[position].set(local_flat)  16.1 us
  transfers between devices with their start and end apart: 5, of which 4 were waited for; matrix products, arithmetic and copies ran while one was open for 11% of the time, Pallas kernels for 0%

commit v1 on v0

v1 whole, which is shorter than its diff:
```python
import functools

import jax
import jax.numpy as jnp
from jax import lax
from jax.experimental import pallas as pl
from jax.experimental.pallas import tpu as pltpu
from jax.sharding import PartitionSpec as P

LEARN = 0.5
EPSILON = 1e-06
F32, BF16, I32 = jnp.float32, jnp.bfloat16, jnp.int32
VMEM = pl.BlockSpec(memory_space=pltpu.VMEM)
SMEM = pl.BlockSpec(memory_space=pltpu.SMEM)
PARAMS = pltpu.CompilerParams(vmem_limit_bytes=48 * 1024 * 1024)


def pack_kernel(rank_ref, grads_ref, rows_ref, out_ref, req_ref):
    owners, bags = rank_ref.shape
    slots = out_ref.shape[1]
    grads = grads_ref[...]
    slot = lax.broadcasted_iota(I32, (slots, bags), 0)

    def one(o, carry):
        hot = slot == rank_ref[pl.ds(o, 1), :]
        out_ref[o] = jnp.dot(
            hot.astype(F32).astype(BF16), grads, preferred_element_type=F32
        ).astype(BF16)
        code = jnp.where(hot, rows_ref[pl.ds(o, 1), :] + 1, 0)
        req_ref[pl.ds(o, 1), :] = jnp.sum(code.T, axis=0, keepdims=True) - 1
        return carry

    lax.fori_loop(0, owners, one, 0)


def pick_kernel(req_ref, table_ref, out_ref, line):
    sources, slots = req_ref.shape

    def one(p, carry):
        for s in range(slots):
            line[pl.ds(s, 1), :] = table_ref[pl.ds(req_ref[p, s], 1), :]
        out_ref[p] = line[...].astype(BF16)
        return carry

    lax.fori_loop(0, sources, one, 0)


def pool_kernel(rank_ref, rows_ref, out_ref, total):
    owners, bags = rank_ref.shape
    slots = rows_ref.shape[1]
    slot = lax.broadcasted_iota(I32, (slots, bags), 0)
    total[...] = jnp.zeros_like(total)

    def one(i, carry):
        hot = jnp.concatenate(
            [slot == rank_ref[pl.ds(2 * i, 1), :], slot == rank_ref[pl.ds(2 * i + 1, 1), :]], axis=0
        )
        rows = jnp.concatenate([rows_ref[2 * i], rows_ref[2 * i + 1]], axis=0)
        total[...] += lax.dot_general(
            rows, hot.astype(F32).astype(BF16), (((0,), (0,)), ((), ())), preferred_element_type=F32
        )
        return carry

    lax.fori_loop(0, owners // 2, one, 0)
    out_ref[...] = total[...].T.astype(BF16)


def add_kernel(req_ref, grads_ref, out_ref, total, chunk=512, group=4):
    sources, slots = req_ref.shape
    rows = total.shape[0]
    total[...] = jnp.zeros_like(total)
    row = lax.broadcasted_iota(I32, (chunk, slots), 0)

    def one(i, carry):
        lines = [req_ref[pl.ds(group * i + k, 1), :] for k in range(group)]
        grads = jnp.concatenate([grads_ref[group * i + k] for k in range(group)], axis=0)
        for c in range(0, rows, chunk):
            hot = jnp.concatenate([row == line - c for line in lines], axis=1)
            total[c : c + chunk, :] += jnp.dot(
                hot.astype(F32).astype(BF16), grads, preferred_element_type=F32
            )
        return carry

    lax.fori_loop(0, sources // group, one, 0)
    out_ref[...] = total[...].astype(BF16)


def place_kernel(code_ref, delta_ref, out_ref, chunk=512):
    count = out_ref.shape[0]
    lines, lanes = code_ref.shape
    slot = lax.broadcasted_iota(I32, (chunk, lanes), 0)
    delta = delta_ref[...]

    def one(i, carry):
        base = pl.multiple_of(i * chunk, chunk)
        hot = jnp.concatenate(
            [slot == code_ref[k : k + 1, :] - base for k in range(lines)], axis=1
        )
        out_ref[pl.ds(base, chunk), :] = jnp.dot(
            hot.astype(F32).astype(BF16), delta, preferred_element_type=F32
        ).astype(BF16)
        return carry

    lax.fori_loop(0, count // chunk, one, 0)


def on_device(owners, local_rows, grad_pooled, table, accum, parity, parity_slot):
    table_count, dp_count = lax.axis_size("table"), lax.axis_size("dp")
    bags, hot = owners.shape
    rows, width = table.shape
    cap = min(bags, 2 * bags * hot // table_count)
    mine = lax.axis_index("dp")

    named = owners.T[:, None, :] == jnp.arange(table_count, dtype=I32)[None, :, None]
    hits = jnp.any(named, axis=0)
    wanted = jnp.sum(jnp.where(named, local_rows.T[:, None, :], 0), axis=0)
    before = jnp.arange(bags)[:, None] < jnp.arange(bags)[None, :]
    rank = jnp.dot(hits.astype(BF16), before.astype(BF16), preferred_element_type=F32)
    rank = jnp.where(hits, rank.astype(I32), -1)

    outgoing, requests = pl.pallas_call(
        pack_kernel,
        out_shape=(
            jax.ShapeDtypeStruct((table_count, cap, width), BF16),
            jax.ShapeDtypeStruct((table_count, cap), I32),
        ),
        in_specs=[VMEM] * 3,
        out_specs=(VMEM, VMEM),
        compiler_params=PARAMS,
        name="pack",
    )(rank, grad_pooled, wanted)
    exchange = functools.partial(
        lax.all_to_all, axis_name="table", split_axis=0, concat_axis=0, tiled=True
    )
    asked = exchange(requests)
    incoming = exchange(outgoing)
    fetched = pl.pallas_call(
        pick_kernel,
        out_shape=jax.ShapeDtypeStruct((table_count, cap, width), BF16),
        in_specs=[SMEM, VMEM],
        out_specs=VMEM,
        scratch_shapes=[pltpu.VMEM((cap, width), F32)],
        compiler_params=PARAMS,
        name="pick",
    )(jnp.maximum(asked, 0), table)
    returned = exchange(fetched)
    partial_grads = pl.pallas_call(
        add_kernel,
        out_shape=jax.ShapeDtypeStruct((rows, width), BF16),
        in_specs=[VMEM] * 2,
        out_specs=VMEM,
        scratch_shapes=[pltpu.VMEM((rows, width), F32)],
        compiler_params=PARAMS,
        name="add",
    )(asked, incoming)
    quarters = lax.all_to_all(
        partial_grads.reshape(dp_count, rows // dp_count, width), "dp", 0, 0, tiled=True
    )
    quarter = jnp.sum(quarters.astype(F32), axis=0).astype(BF16)
    row_grads = lax.all_gather(quarter, "dp", axis=0, tiled=True).astype(F32)
    new_accum = accum + jnp.mean(row_grads * row_grads, axis=1)
    new_table = table - LEARN * row_grads / jnp.sqrt(new_accum + EPSILON)[:, None]
    row_delta = new_table - table

    parity_count = parity.shape[0]
    part = parity_count // dp_count
    holder, place = parity_slot // parity_count, parity_slot % parity_count
    code = jnp.where(place // part == mine, holder * part + place % part, -1)
    spread = pl.pallas_call(
        place_kernel,
        out_shape=jax.ShapeDtypeStruct((table_count * part, width), BF16),
        in_specs=[VMEM] * 2,
        out_specs=VMEM,
        compiler_params=PARAMS,
        name="place",
    )(code.reshape(rows // 128, 128), row_delta.astype(BF16))
    arrived = exchange(spread.reshape(table_count, part, width))
    part_sum = jnp.sum(arrived.astype(F32), axis=0)
    new_parity = parity + lax.all_gather(part_sum, "dp", axis=0, tiled=True)
    pooled = pl.pallas_call(
        pool_kernel,
        out_shape=jax.ShapeDtypeStruct((bags, width), BF16),
        in_specs=[VMEM] * 2,
        out_specs=VMEM,
        scratch_shapes=[pltpu.VMEM((width, bags), F32)],
        compiler_params=PARAMS,
        name="pool",
    )(rank, returned)
    return (pooled, new_table, new_accum, new_parity)


def solution(mesh):
    in_specs = (
        P(("table", "dp"), None),
        P(("table", "dp"), None),
        P(("table", "dp"), None),
        P("table", None),
        P("table"),
        P("table", None),
        P("table"),
    )
    out_specs = (P(("table", "dp"), None), P("table", None), P("table"), P("table", None))
    return jax.shard_map(
        on_device, mesh=mesh, in_specs=in_specs, out_specs=out_specs, check_vma=False
    )
```

time: 399 us -> 239 us (0.60)
  waiting for transfers between devices: 168 us -> 51.1 us
  other arithmetic: 105 us -> 8.56 us
  blocking collectives: 0 us -> 86.4 us
  local copies, waits for them, and re-layouts: 67.9 us -> 2.22 us
  Pallas kernels: 0 us -> 57 us
  starting transfers between devices: 40.2 us -> 18.7 us
    all_to_all x4 -> x3, waiting for transfers between devices: 119 us -> 23 us  [the longest x1 9.5 us: on_device(): returned = exchange(fetched)]
    all_to_all x0 -> x2, blocking collectives: none -> 74.5 us  [the longest x1 54.4 us: on_device(): incoming = exchange(outgoing)]
    pallas_call x0 -> x5, Pallas kernels: none -> 57 us  [the longest x1 21.4 us: on_device(): pl.pallas_call(add_kernel, out_shape=jax.ShapeDtypeStruct((rows, width),...]
    scatter-add x1 -> x0, other arithmetic: 52.6 us -> none  [on_device(): jax.ops.segment_sum(incoming.reshape(slot_count, row_width).astype(jnp.fl...]
    psum x1 -> x0, waiting for transfers between devices: 48.9 us -> none  [on_device(): lax.psum(partial_grads.astype(jnp.bfloat16), 'dp').astype(jnp.float32)]
    gather x2 -> x0, local copies, waits for them, and re-layouts: 36.2 us -> none  [the longest x1 24 us: on_device(): jnp.take(table_half, jnp.minimum(asked_rows, row_count - 1), axis=0)]
    scatter x2 -> x0, local copies, waits for them, and re-layouts: 28.5 us -> none  [the longest x1 16.1 us: on_device(): jnp.full((slot_count,), row_count, jnp.int32).at[position].set(local_flat)]
    all_gather x0 -> x1, waiting for transfers between devices: none -> 28 us  [on_device(): row_grads = lax.all_gather(quarter, 'dp', axis=0, tiled=True).astype(F32)]
  transfers between devices with their start and end apart: 5 -> 4, of which waited for: 4 -> 4; matrix products, arithmetic and copies ran while one was open for 11% -> 3% of each run, Pallas kernels for 0% -> 10%
where the time goes in v1:
time: 239 us; the launch traced here: 238 us
  blocking collectives  86.4 us (36%)
  Pallas kernels  57 us (24%)
  waiting for transfers between devices  51.1 us (21%)
  starting transfers between devices  18.7 us (8%)
  between operations  14.1 us (6%)
  other arithmetic  8.56 us (4%)
    all_to_all x1, blocking collectives, on_device(): incoming = exchange(outgoing)  54.4 us
    all_gather x1, waiting for transfers between devices, on_device(): row_grads = lax.all_gather(quarter, 'dp', axis=0, tiled=True).astype(F32)  28 us
    pallas_call x1, Pallas kernels, on_device(): pl.pallas_call(add_kernel, out_shape=jax.ShapeDtypeStruct((rows, width),...  21.4 us
    all_to_all x1, blocking collectives, on_device(): asked = exchange(requests)  20.1 us
    all_gather x1, blocking collectives, on_device(): new_parity = parity + lax.all_gather(part_sum, 'dp', axis=0, tiled=True)  11.9 us
    pallas_call x1, Pallas kernels, on_device(): pl.pallas_call(pack_kernel, out_shape=(jax.ShapeDtypeStruct((table_count,...  11.8 us
    all_to_all x1, waiting for transfers between devices, on_device(): returned = exchange(fetched)  9.5 us
    pallas_call x1, Pallas kernels, on_device(): pl.pallas_call(pool_kernel, out_shape=jax.ShapeDtypeStruct((bags, width),...  9.18 us
  transfers between devices with their start and end apart: 4, of which 4 were waited for; matrix products, arithmetic and copies ran while one was open for 3% of the time, Pallas kernels for 10%

profile of v1, /device:TPU:32, one launch (start us, length us, event | category | flops | bytes accessed | tf_op | source)
XLA Modules:
  0.0 238.4 jit_solution(13170247127809219251)
XLA Ops:
  7.2 0.9 fusion.4
  8.0 0.2 fusion.3.rank_ref
  8.2 0.9 select_reduce_fusion.rows_ref
  9.1 0.0 copy-start.2
  9.1 0.9 copy-done.2
  10.0 11.8 %pack.1 = (bf16[64,128,128]{2,1,0:T(8,128)(2,1)S(1)}, s32[64,128]{1,0:T(8,128)S(1)}) custom-call(s32[64,512]{1,0:T(8,128)S(1)} %fusion.3.rank_ref, bf16[512,128]{1,0:T(8,128)(2,1)S(1)} %copy-done.2, s32[64,512]{1,0:T(8,128)S(1)} %select_reduce_fusion.rows_ref), custom_call_target="tpu_custom_call" | custom-call | tf_op jit(solution)/shard_map/pack/pallas_call | solution.py:121
  21.8 20.1 %all_to_all.31 = s32[64,1,128]{2,1,0:T(1,128)S(1)} all-to-all(s32[64,1,128]{2,1,0:T(1,128)S(1)} %bitcast.13), channel_id=1, replica_groups=mesh['table'=64,'dp'=4] {'table'}, dimensions={0} | all-to-all | bytes 65536 | tf_op jit(solution)/shard_map/all_to_all | solution.py:135
  41.9 54.4 %all_to_all.32.grads_ref = bf16[64,128,128]{2,1,0:T(8,128)(2,1)S(1)} all-to-all(bf16[64,128,128]{2,1,0:T(8,128)(2,1)S(1)} %get-tuple-element.7), channel_id=1, replica_groups=mesh['table'=64,'dp'=4] {'table'}, dimensions={0} | all-to-all | bytes 4194304 | tf_op jit(solution)/shard_map/all_to_all | solution.py:136
  96.3 0.0 copy-start
  96.3 21.4 %add.50 = bf16[4096,128]{1,0:T(8,128)(2,1)} custom-call(s32[64,128]{1,0:T(8,128)S(1)} %bitcast.11, bf16[64,128,128]{2,1,0:T(8,128)(2,1)S(1)} %all_to_all.32.grads_ref), custom_call_target="tpu_custom_call" | custom-call | tf_op jit(solution)/shard_map/add/pallas_call | solution.py:147
  117.7 4.3 %all-to-all-start.3 = ((bf16[4,1024,128]{2,1,0:T(8,128)(2,1)}), bf16[4,1024,128]{2,1,0:T(8,128)(2,1)S(1)}, u32[]{:S(2)}, u32[]{:S(2)}) async-start(bf16[4,1024,128]{2,1,0:T(8,128)(2,1)} %bitcast.5), calls=%async_computation.3 | async-start | bytes 2097152 | tf_op jit(solution)/shard_map/all_to_all | solution.py:156
  122.0 0.0 copy-done
  122.0 8.8 %pick.1 = bf16[64,128,128]{2,1,0:T(8,128)(2,1)S(1)} custom-call(s32[64,128]{1,0:T(8,128)S(1)} %broadcast_maximum_fusion.req_ref, f32[4096,128]{1,0:T(8,128)S(1)} %copy-done), custom_call_target="tpu_custom_call" | custom-call | tf_op jit(solution)/shard_map/pick/pallas_call | solution.py:137
  130.7 0.0 copy-start.1
  130.8 1.3 copy-done.1
  132.1 0.0 copy-start.4
  132.1 5.6 %all-to-all-done.3 = bf16[4,1024,128]{2,1,0:T(8,128)(2,1)S(1)} async-done(((bf16[4,1024,128]{2,1,0:T(8,128)(2,1)}), bf16[4,1024,128]{2,1,0:T(8,128)(2,1)S(1)}, u32[]{:S(2)}, u32[]{:S(2)}) %all-to-all-start.3) | async-done | bytes 1048608 | tf_op jit(solution)/shard_map/all_to_all | solution.py:156
  137.7 7.1 %all-to-all-start.1 = ((bf16[64,128,128]{2,1,0:T(8,128)(2,1)}), bf16[64,128,128]{2,1,0:T(8,128)(2,1)}, u32[]{:S(2)}, u32[]{:S(2)}) async-start(bf16[64,128,128]{2,1,0:T(8,128)(2,1)} %copy-done.1), calls=%async_computation.1 | async-start | bytes 4194304 | tf_op jit(solution)/shard_map/all_to_all | solution.py:146
  144.8 0.0 copy-start.5
  144.8 0.0 all-gather.2.cloned.1.call-start
  144.9 0.9 reduce_sum.40
  145.8 0.0 all-gather.2.cloned.1.call-update
  145.8 0.0 copy-done.4
  145.9 28.0 %all-gather.2.cloned.1.call-done = bf16[4096,128]{1,0:T(8,128)(2,1)} async-done(((bf16[1024,128]{1,0:T(8,128)(2,1)}), bf16[4096,128]{1,0:T(8,128)(2,1)}) %all-gather.2.cloned.1.call-update) | async-done | bytes 1048592 | tf_op jit(solution)/shard_map/all_gather | solution.py:160
  173.9 1.8 fusion.2
  175.7 0.0 copy-done.5
  175.8 0.6 add_sqrt_fusion
  176.4 2.7 %subtract_convert_fusion = (bf16[4096,128]{1,0:T(8,128)(2,1)S(1)}, f32[4096,128]{1,0:T(8,128)}) fusion(f32[4096,128]{1,0:T(8,128)S(1)} %copy-done, f32[4096]{0:T(1024)S(1)} %get-tuple-element.10, bf16[4096,128]{1,0:T(8,128)(2,1)} %all-gather.2.cloned.1.call-done), kind=kLoop, calls=%fused_computation.5 | loop fusion | flops 3145728 | bytes 6307840 | tf_op jit(solution)/shard_map/convert_element_type | solution.py:176
  179.1 5.9 %place.1 = bf16[2048,128]{1,0:T(8,128)(2,1)} custom-call(s32[32,128]{1,0:T(8,128)S(1)} %fusion.9.code_ref, bf16[4096,128]{1,0:T(8,128)(2,1)S(1)} %get-tuple-element.8.delta_ref), custom_call_target="tpu_custom_call" | custom-call | tf_op jit(solution)/shard_map/place/pallas_call | solution.py:169
  185.0 0.0 copy-start.3
  185.0 9.5 %all-to-all-done.1.rows_ref = bf16[64,128,128]{2,1,0:T(8,128)(2,1)} async-done(((bf16[64,128,128]{2,1,0:T(8,128)(2,1)}), bf16[64,128,128]{2,1,0:T(8,128)(2,1)}, u32[]{:S(2)}, u32[]{:S(2)}) %all-to-all-start.1) | async-done | bytes 2097184 | tf_op jit(solution)/shard_map/all_to_all | solution.py:146
  194.5 7.3 %all-to-all-start.4 = ((bf16[64,32,128]{2,1,0:T(8,128)(2,1)}), bf16[64,32,128]{2,1,0:T(8,128)(2,1)S(1)}, u32[]{:S(2)}, u32[]{:S(2)}) async-start(bf16[64,32,128]{2,1,0:T(8,128)(2,1)} %bitcast.7), calls=%async_computation.4 | async-start | bytes 1048576 | tf_op jit(solution)/shard_map/all_to_all | solution.py:177
  201.8 9.2 %pool.1 = bf16[512,128]{1,0:T(8,128)(2,1)} custom-call(s32[64,512]{1,0:T(8,128)S(1)} %fusion.3.rank_ref, bf16[64,128,128]{2,1,0:T(8,128)(2,1)} %all-to-all-done.1.rows_ref), custom_call_target="tpu_custom_call" | custom-call | tf_op jit(solution)/shard_map/pool/pallas_call | solution.py:180
  211.0 7.9 %all-to-all-done.4 = bf16[64,32,128]{2,1,0:T(8,128)(2,1)S(1)} async-done(((bf16[64,32,128]{2,1,0:T(8,128)(2,1)}), bf16[64,32,128]{2,1,0:T(8,128)(2,1)S(1)}, u32[]{:S(2)}, u32[]{:S(2)}) %all-to-all-start.4) | async-done | bytes 524320 | tf_op jit(solution)/shard_map/all_to_all | solution.py:177
  218.9 0.1 convert_reduce_fusion
  219.0 11.9 %all_gather.7 = f32[128,128]{1,0:T(8,128)S(1)} all-gather(f32[32,128]{1,0:T(8,128)S(1)} %convert_reduce_fusion), channel_id=1, replica_groups=mesh['table'=64,'dp'=4] {'dp'}, dimensions={0}, use_global_device_ids=true | all-gather | bytes 81920 | tf_op jit(solution)/shard_map/all_gather | solution.py:179
  230.9 0.0 copy-done.3
  230.9 0.6 add.34
  (2 shorter events, 0.0 us)
Async XLA Ops:
  9.1 0.9 copy-start.2
  96.3 25.7 %copy-start = (f32[4096,128]{1,0:T(8,128)S(1)}, f32[4096,128]{1,0:T(8,128)}, u32[]{:S(2)}) copy-start(f32[4096,128]{1,0:T(8,128)} %table_ref.1) | copy-start | bytes 6291460
  117.7 20.0 %all-to-all-start.3 = ((bf16[4,1024,128]{2,1,0:T(8,128)(2,1)}), bf16[4,1024,128]{2,1,0:T(8,128)(2,1)S(1)}, u32[]{:S(2)}, u32[]{:S(2)}) async-start(bf16[4,1024,128]{2,1,0:T(8,128)(2,1)} %bitcast.5), calls=%async_computation.3 | async-start | bytes 2097152 | tf_op jit(solution)/shard_map/all_to_all | solution.py:156
  130.7 1.3 copy-start.1
  132.1 13.8 %copy-start.4 = (s32[4096]{0:T(1024)S(1)}, s32[4096]{0:T(1024)}, u32[]{:S(2)}) copy-start(s32[4096]{0:T(1024)} %param.13) | copy-start | bytes 49156
  137.7 56.9 %all-to-all-start.1 = ((bf16[64,128,128]{2,1,0:T(8,128)(2,1)}), bf16[64,128,128]{2,1,0:T(8,128)(2,1)}, u32[]{:S(2)}, u32[]{:S(2)}) async-start(bf16[64,128,128]{2,1,0:T(8,128)(2,1)} %copy-done.1), calls=%async_computation.1 | async-start | bytes 4194304 | tf_op jit(solution)/shard_map/all_to_all | solution.py:146
  144.8 30.9 %copy-start.5 = (f32[4096]{0:T(1024)S(1)}, f32[4096]{0:T(1024)}, u32[]{:S(2)}) copy-start(f32[4096]{0:T(1024)} %param.11) | copy-start | bytes 49156
  144.8 29.1 %all-gather.2.cloned.1.call-start = ((), (), s32[]{:S(2)}) async-start(), calls=%async_computation.5 | async-start | bytes 1310720 | tf_op jit(solution)/shard_map/all_gather | solution.py:160
  185.0 45.8 %copy-start.3 = (f32[128,128]{1,0:T(8,128)S(1)}, f32[128,128]{1,0:T(8,128)}, u32[]{:S(2)}) copy-start(f32[128,128]{1,0:T(8,128)} %param.12) | copy-start | bytes 196612
  194.5 24.4 %all-to-all-start.4 = ((bf16[64,32,128]{2,1,0:T(8,128)(2,1)}), bf16[64,32,128]{2,1,0:T(8,128)(2,1)S(1)}, u32[]{:S(2)}, u32[]{:S(2)}) async-start(bf16[64,32,128]{2,1,0:T(8,128)(2,1)} %bitcast.7), calls=%async_computation.4 | async-start | bytes 1048576 | tf_op jit(solution)/shard_map/all_to_all | solution.py:177
Sparse Core Ops, SparseCore 0:
  148.1 25.7 all-gather.1

commit v2 on v1

v2 whole, which is shorter than its diff:
```python
import functools

import jax
import jax.numpy as jnp
from jax import lax
from jax.experimental import pallas as pl
from jax.experimental.pallas import tpu as pltpu
from jax.sharding import PartitionSpec as P

LEARN = 0.5
EPSILON = 1e-06
F32, BF16, I32 = jnp.float32, jnp.bfloat16, jnp.int32
VMEM = pl.BlockSpec(memory_space=pltpu.VMEM)
MESH = pl.DeviceIdType.MESH
PARAMS = pltpu.CompilerParams(vmem_limit_bytes=48 * 1024 * 1024)


def front_kernel(
    rank_ref, grads_ref, wanted_ref, table_ref, pooled_ref, sums_ref,
    table, g_out, g_in, q_out, q_in, q_line, q_smem, r_out, r_in, total, pool, part, quarter_in,
    line, gs, gr, qs, qr, rs, rr, ps, pr, us, ur, table_sem, q_sem,
):
    n, bags = rank_ref.shape
    slots, width = g_out.shape[1:]
    rows = total.shape[0]
    dp = quarter_in.shape[0]
    quarter = rows // dp
    me, mine = lax.axis_index("table"), lax.axis_index("dp")

    def offset(k):
        j = (k + 1) // 2
        return (k % 2) * j + (1 - k % 2) * (n - j)

    def to(k):
        return (me + offset(k)) % n

    def frm(k):
        return (me + n - offset(k)) % n

    def copy(out, into, send, recv, peer, place):
        return pltpu.make_async_remote_copy(
            src_ref=out.at[peer], dst_ref=into.at[place], send_sem=send.at[peer],
            recv_sem=recv.at[place], device_id={"table": peer}, device_id_type=MESH,
        )

    def dp_to(k):
        return (mine + k) % dp

    def quarter_of(d):
        return pl.ds(pl.multiple_of(d * quarter, quarter), quarter)

    def reduce_copy(peer, place):
        return pltpu.make_async_remote_copy(
            src_ref=part.at[quarter_of(peer)], dst_ref=quarter_in.at[place], send_sem=ps.at[peer],
            recv_sem=pr.at[place], device_id={"dp": peer}, device_id_type=MESH,
        )

    def gather_copy(peer, place):
        return pltpu.make_async_remote_copy(
            src_ref=sums_ref.at[quarter_of(place)], dst_ref=sums_ref.at[quarter_of(place)],
            send_sem=us.at[peer], recv_sem=ur.at[place], device_id={"dp": peer},
            device_id_type=MESH,
        )

    barrier = pltpu.get_barrier_semaphore()

    def greet(k, carry):
        pl.semaphore_signal(barrier, inc=1, device_id={"table": (me + k) % n}, device_id_type=MESH)
        return carry

    lax.fori_loop(1, n, greet, 0)
    for k in range(1, dp):
        pl.semaphore_signal(barrier, inc=1, device_id={"dp": dp_to(k)}, device_id_type=MESH)
    load = pltpu.make_async_copy(table_ref, table.at[0:rows], table_sem)
    load.start()
    table[rows : rows + 8, :] = jnp.zeros((8, width), F32)
    pl.semaphore_wait(barrier, n - 1 + dp - 1)

    slot = lax.broadcasted_iota(I32, (slots, bags), 0)

    def packed(o):
        hot = slot == rank_ref[pl.ds(o, 1), :]
        lines = jnp.dot(hot.astype(F32).astype(BF16), grads_ref[...], preferred_element_type=F32)
        code = jnp.where(hot, wanted_ref[pl.ds(o, 1), :] + 1, 0)
        code = sum(code[:, c : c + slots] for c in range(0, bags, slots))
        code = jnp.sum(code.T, axis=0, keepdims=True)
        code = jnp.where(code == 0, rows, code - 1)
        return lines.astype(BF16), jnp.broadcast_to(code, (8, slots))

    def pack(k, carry):
        o = to(k)
        lines, code = packed(o)
        q_out[o] = code
        copy(q_out, q_in, qs, qr, o, me).start()
        g_out[o] = lines
        copy(g_out, g_in, gs, gr, o, me).start()
        return carry

    lax.fori_loop(1, n, pack, 0)
    lines, code = packed(me)
    g_in[me] = lines
    q_in[me] = code

    def asked(k, carry):
        p = frm(k)
        copy(q_out, q_in, qs, qr, p, p).wait_recv()
        return carry

    lax.fori_loop(1, n, asked, 0)
    for p in range(n):
        q_line[p : p + 1, :] = q_in[p, 0:1, :]
    fetch = pltpu.make_async_copy(q_line, q_smem, q_sem)
    fetch.start()
    fetch.wait()
    load.wait()

    def pick(p):
        for s in range(slots):
            line[pl.ds(s, 1), :] = table[pl.ds(q_smem[p, s], 1), :]
        return line[...].astype(BF16)

    def serve(k, carry):
        p = frm(k)
        r_out[p] = pick(p)
        copy(r_out, r_in, rs, rr, p, me).start()
        return carry

    lax.fori_loop(1, n, serve, 0)
    r_in[me] = pick(me)

    total[...] = jnp.zeros_like(total)
    chunk, group = 512, 4
    row = lax.broadcasted_iota(I32, (chunk, slots), 0)

    def add(i, carry):
        sources = [frm(group * i + j) for j in range(group)]
        for j, p in enumerate(sources):

            def arrive(p=p):
                copy(g_out, g_in, gs, gr, p, p).wait_recv()

            if j == 0:
                pl.when(i > 0)(arrive)
            else:
                arrive()
        lines = [q_line[pl.ds(p, 1), :] for p in sources]
        grads = jnp.concatenate([g_in[p] for p in sources], axis=0)
        for c in range(0, rows, chunk):
            hot = jnp.concatenate([row == one - c for one in lines], axis=1)
            total[c : c + chunk, :] += jnp.dot(
                hot.astype(F32).astype(BF16), grads, preferred_element_type=F32
            )
        return carry

    lax.fori_loop(0, n // group, add, 0)
    part[...] = total[...].astype(BF16)
    for k in range(1, dp):
        reduce_copy(dp_to(k), mine).start()
    summed = total[quarter_of(mine), :].astype(BF16).astype(F32)
    for k in range(1, dp):
        d = dp_to(k)
        reduce_copy(d, d).wait_recv()
        summed = summed + quarter_in[d].astype(F32)
    sums_ref[quarter_of(mine), :] = summed.astype(BF16)
    for k in range(1, dp):
        gather_copy(dp_to(k), mine).start()

    pool[...] = jnp.zeros_like(pool)

    def gather(i, carry):
        sources = [frm(2 * i), frm(2 * i + 1)]

        @pl.when(i > 0)
        def _():
            copy(r_out, r_in, rs, rr, sources[0], sources[0]).wait_recv()

        copy(r_out, r_in, rs, rr, sources[1], sources[1]).wait_recv()
        hot = jnp.concatenate([slot == rank_ref[pl.ds(o, 1), :] for o in sources], axis=0)
        lines = jnp.concatenate([r_in[o] for o in sources], axis=0)
        pool[...] += lax.dot_general(
            lines, hot.astype(F32).astype(BF16), (((0,), (0,)), ((), ())),
            preferred_element_type=F32,
        )
        return carry

    lax.fori_loop(0, n // 2, gather, 0)
    pooled_ref[...] = pool[...].T.astype(BF16)

    def sent(k, carry):
        p = to(k)
        copy(q_out, q_in, qs, qr, p, me).wait_send()
        copy(g_out, g_in, gs, gr, p, me).wait_send()
        copy(r_out, r_in, rs, rr, p, me).wait_send()
        return carry

    lax.fori_loop(1, n, sent, 0)
    for k in range(1, dp):
        d = dp_to(k)
        reduce_copy(d, mine).wait_send()
        gather_copy(d, d).wait_recv()
        gather_copy(d, mine).wait_send()


def front(rank, grads, wanted, table, dp):
    n, bags = rank.shape
    rows, width = table.shape
    cap = min(bags, 128)
    dma = pltpu.SemaphoreType.DMA
    blocks = pltpu.VMEM((n, cap, width), BF16)
    return pl.pallas_call(
        front_kernel,
        out_shape=(
            jax.ShapeDtypeStruct((bags, width), BF16),
            jax.ShapeDtypeStruct((rows, width), BF16),
        ),
        in_specs=[VMEM, VMEM, VMEM, pl.BlockSpec(memory_space=pl.ANY)],
        out_specs=(VMEM, VMEM),
        scratch_shapes=[
            pltpu.VMEM((rows + 8, width), F32),
            blocks,
            blocks,
            pltpu.VMEM((n, 8, cap), I32),
            pltpu.VMEM((n, 8, cap), I32),
            pltpu.VMEM((n, cap), I32),
            pltpu.SMEM((n, cap), I32),
            blocks,
            blocks,
            pltpu.VMEM((rows, width), F32),
            pltpu.VMEM((width, bags), F32),
            pltpu.VMEM((rows, width), BF16),
            pltpu.VMEM((dp, rows // dp, width), BF16),
            pltpu.VMEM((cap, width), F32),
        ]
        + [dma((n,))] * 6
        + [dma((dp,))] * 4
        + [dma, dma],
        compiler_params=pltpu.CompilerParams(
            vmem_limit_bytes=48 * 1024 * 1024, collective_id=0, has_side_effects=True
        ),
        name="front",
    )(rank, grads, wanted, table)


def place_kernel(code_ref, delta_ref, out_ref, chunk=512):
    count = out_ref.shape[0]
    lines, lanes = code_ref.shape
    slot = lax.broadcasted_iota(I32, (chunk, lanes), 0)
    delta = delta_ref[...]

    def one(i, carry):
        base = pl.multiple_of(i * chunk, chunk)
        hot = jnp.concatenate(
            [slot == code_ref[k : k + 1, :] - base for k in range(lines)], axis=1
        )
        out_ref[pl.ds(base, chunk), :] = jnp.dot(
            hot.astype(F32).astype(BF16), delta, preferred_element_type=F32
        ).astype(BF16)
        return carry

    lax.fori_loop(0, count // chunk, one, 0)


def on_device(owners, local_rows, grad_pooled, table, accum, parity, parity_slot):
    table_count, dp_count = lax.axis_size("table"), lax.axis_size("dp")
    bags, hot = owners.shape
    rows, width = table.shape
    mine = lax.axis_index("dp")

    named = owners.T[:, None, :] == jnp.arange(table_count, dtype=I32)[None, :, None]
    hits = jnp.any(named, axis=0)
    wanted = jnp.sum(jnp.where(named, local_rows.T[:, None, :], 0), axis=0)
    before = jnp.arange(bags)[:, None] < jnp.arange(bags)[None, :]
    rank = jnp.dot(hits.astype(BF16), before.astype(BF16), preferred_element_type=F32)
    rank = jnp.where(hits, rank.astype(I32), -1)

    pooled, sums = front(rank, grad_pooled, wanted, table, dp_count)
    row_grads = sums.astype(F32)
    exchange = functools.partial(
        lax.all_to_all, axis_name="table", split_axis=0, concat_axis=0, tiled=True
    )
    new_accum = accum + jnp.mean(row_grads * row_grads, axis=1)
    new_table = table - LEARN * row_grads / jnp.sqrt(new_accum + EPSILON)[:, None]
    row_delta = new_table - table

    parity_count = parity.shape[0]
    part = parity_count // dp_count
    holder, place = parity_slot // parity_count, parity_slot % parity_count
    code = jnp.where(place // part == mine, holder * part + place % part, -1)
    spread = pl.pallas_call(
        place_kernel,
        out_shape=jax.ShapeDtypeStruct((table_count * part, width), BF16),
        in_specs=[VMEM] * 2,
        out_specs=VMEM,
        compiler_params=PARAMS,
        name="place",
    )(code.reshape(rows // 128, 128), row_delta.astype(BF16))
    arrived = exchange(spread.reshape(table_count, part, width))
    part_sum = jnp.sum(arrived.astype(F32), axis=0)
    new_parity = parity + lax.all_gather(part_sum, "dp", axis=0, tiled=True)
    return (pooled, new_table, new_accum, new_parity)


def solution(mesh):
    in_specs = (
        P(("table", "dp"), None),
        P(("table", "dp"), None),
        P(("table", "dp"), None),
        P("table", None),
        P("table"),
        P("table", None),
        P("table"),
    )
    out_specs = (P(("table", "dp"), None), P("table", None), P("table"), P("table", None))
    return jax.shard_map(
        on_device, mesh=mesh, in_specs=in_specs, out_specs=out_specs, check_vma=False
    )
```

time: 239 us -> 178 us (0.74)
  Pallas kernels: 57 us -> 132 us
  blocking collectives: 86.4 us -> 11.9 us
  waiting for transfers between devices: 51.1 us -> 17.1 us
  between operations: 14.1 us -> 0.7 us
  starting transfers between devices: 18.7 us -> 6.87 us
  other arithmetic: 8.56 us -> 5.38 us
    pallas_call x4 -> x1, Pallas kernels: 51.1 us -> 126 us  [front(): pl.pallas_call(front_kernel, out_shape=(jax.ShapeDtypeStruct((bags, width...]
    all_to_all x2 -> x0, blocking collectives: 74.5 us -> none  [the longest x1 54.4 us: on_device(): incoming = exchange(outgoing)]
    all_gather x1 -> x0, waiting for transfers between devices: 28 us -> none  [on_device(): row_grads = lax.all_gather(quarter, 'dp', axis=0, tiled=True).astype(F32)]
    all_to_all x2 -> x0, waiting for transfers between devices: 15.1 us -> none  [the longest x1 9.5 us: on_device(): returned = exchange(fetched)]
    all_to_all x2 -> x0, starting transfers between devices: 11.4 us -> none  [the longest x1 7.14 us: on_device(): returned = exchange(fetched)]
    all_to_all x1, waiting for transfers between devices: 7.93 us -> 17.1 us  [on_device(): arrived = exchange(spread.reshape(table_count, part, width))]
  transfers between devices with their start and end apart: 4 -> 1, of which waited for: 4 -> 1; matrix products, arithmetic and copies ran while one was open for 3% -> 0% of each run, Pallas kernels for 10% -> 0%
where the time goes in v2:
time: 178 us
  Pallas kernels  132 us (74%)
  waiting for transfers between devices  17.1 us (10%)
  blocking collectives  11.9 us (7%)
  starting transfers between devices  6.87 us (4%)
  other arithmetic  5.38 us (3%)
  local copies, waits for them, and re-layouts  3.16 us (2%)
    pallas_call x1, Pallas kernels, front(): pl.pallas_call(front_kernel, out_shape=(jax.ShapeDtypeStruct((bags, width...  126 us
    all_to_all x1, waiting for transfers between devices, on_device(): arrived = exchange(spread.reshape(table_count, part, width))  17.1 us
    all_gather x1, blocking collectives, on_device(): new_parity = parity + lax.all_gather(part_sum, 'dp', axis=0, tiled=True)  11.9 us
    all_to_all x1, starting transfers between devices, on_device(): arrived = exchange(spread.reshape(table_count, part, width))  6.87 us
    pallas_call x1, Pallas kernels, on_device(): pl.pallas_call(place_kernel, out_shape=jax.ShapeDtypeStruct((table_count...  5.93 us
  transfers between devices with their start and end apart: 1, of which 1 were waited for; matrix products, arithmetic and copies ran while one was open for 0% of the time, Pallas kernels for 0%

profile of v2, /device:TPU:32, one launch (start us, length us, event | category | flops | bytes accessed | tf_op | source)
XLA Modules:
  0.0 177.7 jit_solution(5544995632412689023)
XLA Ops:
  0.6 0.9 fusion.4
  1.5 0.0 copy-start.4
  1.5 0.2 fusion.3.rank_ref
  1.7 0.9 select_reduce_fusion.wanted_ref
  2.6 0.0 copy-start
  2.6 1.6 copy-done
  4.2 0.0 copy-start.1
  4.2 0.9 copy-done.1
  5.1 126.5 %front.1 = (bf16[512,128]{1,0:T(8,128)(2,1)S(1)}, bf16[4096,128]{1,0:T(8,128)(2,1)S(1)}) custom-call(s32[64,512]{1,0:T(8,128)S(1)} %fusion.3.rank_ref, bf16[512,128]{1,0:T(8,128)(2,1)S(1)} %copy-done.1, s32[64,512]{1,0:T(8,128)S(1)} %select_reduce_fusion.wanted_ref, f32[4096,128]{1,0:T(8,128)S(1)} %copy-done), custom_call_target="tpu_custom_call" | custom-call | tf_op jit(solution)/shard_map/front/pallas_call | solution.py:210
  131.6 0.6 fusion.2
  132.2 0.0 copy-done.4
  132.2 0.6 add_sqrt_fusion
  132.8 0.0 copy-start.3
  132.8 1.7 subtract_convert_fusion
  134.5 0.0 copy-start.2
  134.5 0.0 copy-done.3
  134.5 5.9 %place.1 = bf16[2048,128]{1,0:T(8,128)(2,1)} custom-call(s32[32,128]{1,0:T(8,128)S(1)} %fusion.9.code_ref, bf16[4096,128]{1,0:T(8,128)(2,1)S(1)} %get-tuple-element.8.delta_ref), custom_call_target="tpu_custom_call" | custom-call | tf_op jit(solution)/shard_map/place/pallas_call | solution.py:289
  140.4 6.9 %all-to-all-start = ((bf16[64,32,128]{2,1,0:T(8,128)(2,1)}), bf16[64,32,128]{2,1,0:T(8,128)(2,1)S(1)}, u32[]{:S(2)}, u32[]{:S(2)}) async-start(bf16[64,32,128]{2,1,0:T(8,128)(2,1)} %bitcast.3), calls=%async_computation | async-start | bytes 1048576 | tf_op jit(solution)/shard_map/all_to_all | solution.py:297
  147.3 17.1 %all-to-all-done = bf16[64,32,128]{2,1,0:T(8,128)(2,1)S(1)} async-done(((bf16[64,32,128]{2,1,0:T(8,128)(2,1)}), bf16[64,32,128]{2,1,0:T(8,128)(2,1)S(1)}, u32[]{:S(2)}, u32[]{:S(2)}) %all-to-all-start) | async-done | bytes 524320 | tf_op jit(solution)/shard_map/all_to_all | solution.py:297
  164.4 0.1 convert_reduce_fusion
  164.5 11.9 %all_gather.3 = f32[128,128]{1,0:T(8,128)S(1)} all-gather(f32[32,128]{1,0:T(8,128)S(1)} %convert_reduce_fusion), channel_id=1, replica_groups=mesh['table'=64,'dp'=4] {'dp'}, dimensions={0}, use_global_device_ids=true | all-gather | bytes 81920 | tf_op jit(solution)/shard_map/all_gather | solution.py:299
  176.4 0.0 copy-done.2
  176.4 0.6 add.33
  177.1 0.7 copy.12
  (1 shorter events, 0.0 us)
Async XLA Ops:
  1.5 130.7 %copy-start.4 = (f32[4096]{0:T(1024)S(1)}, f32[4096]{0:T(1024)}, u32[]{:S(2)}) copy-start(f32[4096]{0:T(1024)} %param.11) | copy-start | bytes 49156
  2.6 1.6 copy-start
  4.2 0.9 copy-start.1
  132.8 1.7 copy-start.3
  134.5 42.0 %copy-start.2 = (f32[128,128]{1,0:T(8,128)S(1)}, f32[128,128]{1,0:T(8,128)}, u32[]{:S(2)}) copy-start(f32[128,128]{1,0:T(8,128)} %param.12) | copy-start | bytes 196612
  140.4 24.0 %all-to-all-start = ((bf16[64,32,128]{2,1,0:T(8,128)(2,1)}), bf16[64,32,128]{2,1,0:T(8,128)(2,1)S(1)}, u32[]{:S(2)}, u32[]{:S(2)}) async-start(bf16[64,32,128]{2,1,0:T(8,128)(2,1)} %bitcast.3), calls=%async_computation | async-start | bytes 1048576 | tf_op jit(solution)/shard_map/all_to_all | solution.py:297

commit v3 on v0

v3 whole, which is shorter than its diff:
```python
import jax
import jax.numpy as jnp
from jax import lax
from jax.experimental import pallas as pl
from jax.experimental.pallas import tpu as pltpu
from jax.sharding import PartitionSpec as P

LEARN = 0.5
EPSILON = 1e-06
F32, BF16, I32 = jnp.float32, jnp.bfloat16, jnp.int32
VMEM = pl.BlockSpec(memory_space=pltpu.VMEM)
MESH = pl.DeviceIdType.MESH
NY, NZ, NC = 4, 8, 2
NQ = NY * NC
CAP = 128
HALVES = 2


def near(k):
    j = (k + 1) // 2
    return (k % 2) * j + (1 - k % 2) * ((NZ - j) % NZ)


def step_kernel(
    code_ref, grads_ref, table_ref, accum_ref, slot_ref, parity_ref,
    pooled_ref, new_table_ref, new_accum_ref, new_parity_ref,
    table, wide_accum, line_in, code_in, marks, g_out, g_in, q_out, q_in, q_smem, r_out, r_in,
    total, part, quarter_in, sums, pool_out, pool_in, line, placed, core_out, core_in,
    z_out, z_in, y_out, y_in, x_part,
    code_s, code_r, line_s, line_r, g_s, g_r, q_s, q_r, r_s, r_r, part_s, part_r, sum_s, sum_r,
    pool_s, pool_r, core_s, core_r, z_s, z_r, y_s, y_r, x_s, x_r, table_sem, smem_sem,
):
    bags = code_ref.shape[2]
    rows, width = table_ref.shape
    dp = sums.shape[0]
    quarter = rows // dp
    half = quarter // HALVES
    me, mine = lax.axis_index("table"), lax.axis_index("dp")
    z, c, y = (me // NC) % NZ, me % NC, me // (NC * NZ)
    q = y * NC + c

    def remote(src, dst, send, recv, **where):
        return pltpu.make_async_remote_copy(
            src_ref=src, dst_ref=dst, send_sem=send, recv_sem=recv, device_id=where,
            device_id_type=MESH,
        )

    def on_line(other):
        return (me - z * NC) + other * NC

    def on_plane(other):
        return (other // NC) * (NZ * NC) + z * NC + other % NC

    def code_copy(peer, place):
        return remote(code_ref.at[peer], code_in.at[place], code_s.at[peer], code_r.at[place],
                      table=on_line(peer))

    def line_copy(peer, place):
        return remote(grads_ref, line_in.at[place], line_s.at[peer], line_r.at[place],
                      table=on_line(peer))

    def g_copy(peer, place, s):
        return remote(g_out.at[peer, s], g_in.at[place, s], g_s.at[peer, s], g_r.at[place, s],
                      table=on_plane(peer))

    def q_rows(o):
        return pl.ds(pl.multiple_of(o * NZ, NZ), NZ)

    def q_copy(peer, place):
        return remote(q_out.at[q_rows(peer)], q_in.at[q_rows(place)], q_s.at[peer], q_r.at[place],
                      table=on_plane(peer))

    def r_rows(o):
        return pl.ds(pl.multiple_of(o * CAP, CAP), CAP)

    def r_copy(peer, place, s):
        return remote(r_out.at[peer, s], r_in.at[s, r_rows(place)], r_s.at[peer, s],
                      r_r.at[place, s], table=on_plane(peer))

    def half_rows(h):
        return pl.ds(h * half, half)

    def part_copy(peer, place, h):
        return remote(part.at[peer, half_rows(h)], quarter_in.at[place, half_rows(h)],
                      part_s.at[peer, h], part_r.at[place, h], dp=peer)

    def sum_copy(peer, place, h):
        return remote(sums.at[place, half_rows(h)], sums.at[place, half_rows(h)],
                      sum_s.at[peer, h], sum_r.at[place, h], dp=peer)

    def pool_copy(peer, place):
        return remote(pool_out.at[peer], pool_in.at[place], pool_s.at[peer], pool_r.at[place],
                      table=on_line(peer))

    def core_copy():
        return remote(core_out, core_in, core_s, core_r, table=me + 1 - 2 * c)

    def z_copy(peer, place):
        return remote(z_out.at[peer], z_in.at[place], z_s.at[peer], z_r.at[place],
                      table=on_line(peer))

    def y_copy(peer, place):
        return remote(y_out.at[peer], y_in.at[place], y_s.at[peer], y_r.at[place],
                      table=on_plane(peer * NC + c))

    def x_copy(peer, place):
        return remote(x_part.at[place], x_part.at[place], x_s.at[peer], x_r.at[place], dp=peer)

    line_peers = [(z + near(k)) % NZ for k in range(1, NZ)]
    line_from = [(z + NZ - near(k)) % NZ for k in range(1, NZ)]
    plane_peers = [(q + k) % NQ for k in range(1, NQ)]
    dp_peers = [(mine + k) % dp for k in (1, 3, 2)]
    y_peers = [(y + k) % NY for k in (1, 3, 2)]

    load = pltpu.make_async_copy(table_ref, table.at[0:rows], table_sem)
    load.start()
    barrier = pltpu.get_barrier_semaphore()
    for peer in line_peers:
        pl.semaphore_signal(barrier, inc=1, device_id={"table": on_line(peer)}, device_id_type=MESH)
    for peer in plane_peers:
        pl.semaphore_signal(barrier, inc=1, device_id={"table": on_plane(peer)}, device_id_type=MESH)
    for peer in dp_peers:
        pl.semaphore_signal(barrier, inc=1, device_id={"dp": peer}, device_id_type=MESH)
    table[rows : rows + 8, :] = jnp.zeros((8, width), F32)
    total[...] = jnp.zeros_like(total)
    placed[...] = jnp.zeros_like(placed)

    def widen(i, carry):
        block = jnp.broadcast_to(accum_ref[pl.ds(i, 1), :], (128, 128))
        wide_accum[pl.ds(pl.multiple_of(i * 128, 128), 128), :] = block.T
        return carry

    lax.fori_loop(0, rows // 128, widen, 0)
    pl.semaphore_wait(barrier, len(line_peers) + len(plane_peers) + len(dp_peers))

    for peer in line_peers:
        code_copy(peer, z).start()
    for peer in line_peers:
        line_copy(peer, z).start()
    code_in[z] = code_ref[z]
    line_in[z] = grads_ref[...]

    slot = lax.broadcasted_iota(I32, (CAP, bags), 0)

    def pack(i, carry):
        s = (z + NZ - near(i)) % NZ

        @pl.when(i > 0)
        def _():
            code_copy(s, s).wait_recv()
            line_copy(s, s).wait_recv()

        grads = line_in[s]
        for k in range(1, NQ + 1):
            o = (q + k) % NQ
            code = code_in[s, pl.ds(o, 1), :]
            hot = slot == jnp.where(code < 0, -1, code & (CAP - 1))
            mark = hot.astype(F32).astype(BF16)
            marks[s, r_rows(o), :] = mark
            lines = jnp.dot(mark, grads, preferred_element_type=F32).astype(BF16)
            named = jnp.where(hot, (code >> 7) + 1, 0)
            named = sum(named[:, b : b + CAP] for b in range(0, bags, CAP))
            named = jnp.sum(named.T, axis=0, keepdims=True)
            named = jnp.where(named == 0, rows, named - 1)
            if k < NQ:
                q_out[pl.ds(o * NZ + s, 1), :] = named
                g_out[o, s] = lines
                g_copy(o, q, s).start()
            else:
                q_in[pl.ds(o * NZ + s, 1), :] = named
                g_in[o, s] = lines
        return carry

    lax.fori_loop(0, NZ, pack, 0)
    for peer in plane_peers:
        q_copy(peer, q).start()
    for peer in plane_peers:
        q_copy(peer, peer).wait_recv()
    fetch = pltpu.make_async_copy(q_in, q_smem, smem_sem)
    fetch.start()
    fetch.wait()
    load.wait()

    def pick(o, s):
        for i in range(CAP):
            line[pl.ds(i, 1), :] = table[pl.ds(q_smem[o * NZ + s, i], 1), :]
        return line[...].astype(BF16)

    def serve(i, carry):
        s = (z + near(NZ - 1 - i // NQ)) % NZ
        k = i % NQ
        o = (q + k) % NQ
        picked = pick(o, s)

        @pl.when(k == 0)
        def _():
            r_in[s, r_rows(o), :] = picked

        @pl.when(k > 0)
        def _():
            r_out[o, s] = picked
            r_copy(o, q, s).start()

        return carry

    lax.fori_loop(0, NZ * NQ, serve, 0)

    chunk = 256
    low_row = lax.broadcasted_iota(I32, (chunk, CAP), 0)

    def add(k, carry):
        o = (q + NQ - k) % NQ

        @pl.when(k > 0)
        def _():
            for s in range(NZ):
                g_copy(o, o, s).wait_recv()

        names = q_in[q_rows(o), :]
        low = names & (quarter - 1)
        high = (names // quarter).T
        grads = []
        for s in range(NZ):
            block = jnp.broadcast_to(high[:, s : s + 1], (CAP, width))
            mine_only = [(block == d).astype(F32).astype(BF16) * g_in[o, s] for d in range(dp)]
            grads.append(jnp.concatenate(mine_only, axis=1))
        grads = jnp.concatenate(grads, axis=0)
        for b in range(0, quarter, chunk):
            hot = jnp.concatenate(
                [(low_row == low[s : s + 1, :] - b).astype(F32).astype(BF16) for s in range(NZ)],
                axis=1,
            )
            total[b : b + chunk, :] += jnp.dot(hot, grads, preferred_element_type=F32)
        return carry

    lax.fori_loop(0, NQ, add, 0)
    for h in range(HALVES):
        for d in range(dp):
            part[d, half_rows(h), :] = total[half_rows(h), d * width : (d + 1) * width].astype(BF16)
        for peer in dp_peers:
            part_copy(peer, mine, h).start()

    def pool(i, carry):
        s = (z + near(NZ - 1 - i)) % NZ
        for k in range(1, NQ):
            o = (q + k) % NQ
            r_copy(o, o, s).wait_recv()
        pooled = lax.dot_general(
            r_in[s], marks[s], (((0,), (0,)), ((), ())), preferred_element_type=F32
        )
        pool_out[s] = pooled.astype(BF16)
        pool_copy(s, z).start()
        return carry

    for h in range(HALVES):
        summed = part[mine, half_rows(h), :].astype(F32)
        for peer in dp_peers:
            part_copy(peer, peer, h).wait_recv()
            summed = summed + quarter_in[peer, half_rows(h), :].astype(F32)
        sums[mine, half_rows(h), :] = summed.astype(BF16)
        for peer in dp_peers:
            sum_copy(peer, mine, h).start()

    lax.fori_loop(0, 4, pool, 0)

    slots = placed.shape[0]
    place_chunk = 256
    place_row = lax.broadcasted_iota(I32, (place_chunk, 128), 0)

    def update(d, h):
        base = pl.multiple_of(d * quarter + h * half, half)
        there = pl.ds(base, half)
        g = sums[d, half_rows(h), :].astype(F32)
        squares = jnp.sum(g * g, axis=1, keepdims=True) * (1.0 / width)
        accum = wide_accum[there, :] + squares
        wide_accum[there, :] = accum
        delta = g * (-LEARN) * lax.rsqrt(accum + EPSILON)
        new_table_ref[there, :] = table[there, :] + delta
        delta = delta.astype(BF16)
        lines = [slot_ref[pl.ds(base // 128 + i, 1), :] for i in range(half // 128)]
        for b in range(0, slots, place_chunk):
            hot = jnp.concatenate(
                [(place_row == one - b).astype(F32).astype(BF16) for one in lines], axis=1
            )
            placed[b : b + place_chunk, :] += jnp.dot(hot, delta, preferred_element_type=F32)

    for h in range(HALVES):
        update(mine, h)
    for h in range(HALVES):
        for peer in dp_peers:
            sum_copy(peer, peer, h).wait_recv()
            update(peer, h)

    per_core = slots // NC
    core_out[...] = placed[pl.ds(pl.multiple_of((1 - c) * per_core, per_core), per_core), :].astype(BF16)
    core_copy().start()
    kept = pl.ds(pl.multiple_of(c * per_core, per_core), per_core)
    core_copy().wait_recv()
    placed[kept, :] = placed[kept, :] + core_in[...].astype(F32)
    per_z = per_core // NZ
    for peer in line_peers:
        begin = pl.multiple_of(c * per_core + peer * per_z, per_z)
        z_out[peer] = placed[pl.ds(begin, per_z), :].astype(BF16)
        z_copy(peer, z).start()
    z_sum = placed[pl.ds(pl.multiple_of(c * per_core + z * per_z, per_z), per_z), :]
    lax.fori_loop(4, NZ - 1, pool, 0)
    for k in range(1, NQ):
        o = (q + k) % NQ
        r_copy(o, o, z).wait_recv()
    own_pool = lax.dot_general(
        r_in[z], marks[z], (((0,), (0,)), ((), ())), preferred_element_type=F32
    )
    for peer in line_from:
        z_copy(peer, peer).wait_recv()
        z_sum = z_sum + z_in[peer].astype(F32)
    per_y = per_z // NY
    for j in range(NY):
        y_in[NY + j] = z_sum[j * per_y : (j + 1) * per_y, :]
    for peer in y_peers:
        y_out[peer] = y_in[NY + peer]
        y_copy(peer, y).start()
    y_sum = y_in[NY + y]
    for peer in y_peers:
        y_copy(peer, peer).wait_recv()
        y_sum = y_sum + y_in[peer]
    x_part[mine] = y_sum
    for peer in dp_peers:
        x_copy(peer, mine).start()

    for peer in line_from:
        pool_copy(peer, peer).wait_recv()
        own_pool = own_pool + pool_in[peer].astype(F32)
    pooled_ref[...] = own_pool.T.astype(BF16)

    def narrow(i, carry):
        block = wide_accum[pl.ds(pl.multiple_of(i * 128, 128), 128), :]
        new_accum_ref[pl.ds(i, 1), :] = block.T[0:1, :]
        return carry

    lax.fori_loop(0, rows // 128, narrow, 0)
    for peer in dp_peers:
        x_copy(peer, peer).wait_recv()
    for d in range(dp):
        lines = slice(d * per_y, (d + 1) * per_y)
        new_parity_ref[lines, :] = parity_ref[lines, :] + x_part[d]

    core_copy().wait_send()
    for peer in line_peers:
        code_copy(peer, z).wait_send()
        line_copy(peer, z).wait_send()
        pool_copy(peer, z).wait_send()
        z_copy(peer, z).wait_send()

    def sent(k, carry):
        peer = (q + k) % NQ
        for s in range(NZ):
            g_copy(peer, q, s).wait_send()
            r_copy(peer, q, s).wait_send()
        q_copy(peer, q).wait_send()
        return carry

    lax.fori_loop(1, NQ, sent, 0)
    for peer in dp_peers:
        for h in range(HALVES):
            part_copy(peer, mine, h).wait_send()
            sum_copy(peer, mine, h).wait_send()
        x_copy(peer, mine).wait_send()
    for peer in y_peers:
        y_copy(peer, y).wait_send()


def on_device(owners, local_rows, grad_pooled, table, accum, parity, parity_slot):
    table_count, dp = lax.axis_size("table"), lax.axis_size("dp")
    bags = owners.shape[0]
    rows, width = table.shape
    mine = lax.axis_index("dp")

    index = jnp.arange(table_count, dtype=I32)
    owner_at = (index % NQ // NC * NZ + index // NQ) * NC + index % NC
    named = owners.T[:, None, :] == owner_at[None, :, None]
    hits = jnp.any(named, axis=0)
    wanted = jnp.sum(jnp.where(named, local_rows.T[:, None, :], 0), axis=0)
    before = jnp.arange(bags)[:, None] < jnp.arange(bags)[None, :]
    rank = jnp.dot(hits.astype(BF16), before.astype(BF16), preferred_element_type=F32)
    code = jnp.where(hits, wanted * CAP + rank.astype(I32), -1).reshape(NZ, NQ, bags)

    count = parity.shape[0]
    share = count // dp
    holder, place = parity_slot // count, parity_slot % count
    holder_y, holder_z, holder_c = holder // (NZ * NC), holder // NC % NZ, holder % NC
    order = (holder_c * NZ + holder_z) * NY + holder_y
    slot = jnp.where(place // share == mine, order * share + place % share, -1)
    slots = table_count * share

    quarter = rows // dp
    dma = pltpu.SemaphoreType.DMA
    pooled, new_table, new_accum, new_parity = pl.pallas_call(
        step_kernel,
        out_shape=(
            jax.ShapeDtypeStruct((bags, width), BF16),
            jax.ShapeDtypeStruct((rows, width), F32),
            jax.ShapeDtypeStruct((rows // 128, 128), F32),
            jax.ShapeDtypeStruct((count, width), F32),
        ),
        in_specs=[VMEM, VMEM, pl.BlockSpec(memory_space=pl.ANY), VMEM, VMEM, VMEM],
        out_specs=(VMEM,) * 4,
        scratch_shapes=[
            pltpu.VMEM((rows + 8, width), F32),
            pltpu.VMEM((rows, 128), F32),
            pltpu.VMEM((NZ, bags, width), BF16),
            pltpu.VMEM((NZ, NQ, bags), I32),
            pltpu.VMEM((NZ, NQ * CAP, bags), BF16),
            pltpu.VMEM((NQ, NZ, CAP, width), BF16),
            pltpu.VMEM((NQ, NZ, CAP, width), BF16),
            pltpu.VMEM((NQ * NZ, CAP), I32),
            pltpu.VMEM((NQ * NZ, CAP), I32),
            pltpu.SMEM((NQ * NZ, CAP), I32),
            pltpu.VMEM((NQ, NZ, CAP, width), BF16),
            pltpu.VMEM((NZ, NQ * CAP, width), BF16),
            pltpu.VMEM((quarter, dp * width), F32),
            pltpu.VMEM((dp, quarter, width), BF16),
            pltpu.VMEM((dp, quarter, width), BF16),
            pltpu.VMEM((dp, quarter, width), BF16),
            pltpu.VMEM((NZ, width, bags), BF16),
            pltpu.VMEM((NZ, width, bags), BF16),
            pltpu.VMEM((CAP, width), F32),
            pltpu.VMEM((slots, width), F32),
            pltpu.VMEM((slots // NC, width), BF16),
            pltpu.VMEM((slots // NC, width), BF16),
            pltpu.VMEM((NZ, NY * share, width), BF16),
            pltpu.VMEM((NZ, NY * share, width), BF16),
            pltpu.VMEM((NY, share, width), F32),
            pltpu.VMEM((2 * NY, share, width), F32),
            pltpu.VMEM((dp, share, width), F32),
        ]
        + [dma((NZ,))] * 4
        + [dma((NQ, NZ))] * 2
        + [dma((NQ,))] * 2
        + [dma((NQ, NZ))] * 2
        + [dma((dp, HALVES))] * 4
        + [dma((NZ,))] * 2
        + [dma] * 2
        + [dma((NZ,))] * 2
        + [dma((NY,))] * 2
        + [dma((dp,))] * 2
        + [dma, dma],
        compiler_params=pltpu.CompilerParams(
            vmem_limit_bytes=56 * 1024 * 1024, collective_id=0, has_side_effects=True
        ),
        name="step",
    )(
        code,
        grad_pooled,
        table,
        accum.reshape(rows // 128, 128),
        slot.reshape(rows // 128, 128),
        parity,
    )
    return (pooled, new_table, new_accum.reshape(rows), new_parity)


def solution(mesh):
    in_specs = (
        P(("table", "dp"), None),
        P(("table", "dp"), None),
        P(("table", "dp"), None),
        P("table", None),
        P("table"),
        P("table", None),
        P("table"),
    )
    out_specs = (P(("table", "dp"), None), P("table", None), P("table"), P("table", None))
    return jax.shard_map(
        on_device, mesh=mesh, in_specs=in_specs, out_specs=out_specs, check_vma=False
    )
```

time: 399 us -> 133 us (0.33); the launches traced: 395 us -> 133 us
  waiting for transfers between devices: 168 us -> 0 us
  Pallas kernels: 0 us -> 122 us
  other arithmetic: 105 us -> 3.23 us
  local copies, waits for them, and re-layouts: 67.9 us -> 5.89 us
  starting transfers between devices: 40.2 us -> 0 us
  between operations: 14.2 us -> 0.66 us
    pallas_call x0 -> x1, Pallas kernels: none -> 122 us  [on_device(): pl.pallas_call(step_kernel, out_shape=(jax.ShapeDtypeStruct((bags, width)...]
    all_to_all x4 -> x0, waiting for transfers between devices: 119 us -> none  [the longest x1 49.7 us: on_device(): lax.all_to_all(outgoing.reshape(table_count, capacity, row_width), 'table...]
    scatter-add x1 -> x0, other arithmetic: 52.6 us -> none  [on_device(): jax.ops.segment_sum(incoming.reshape(slot_count, row_width).astype(jnp.fl...]
    psum x1 -> x0, waiting for transfers between devices: 48.9 us -> none  [on_device(): lax.psum(partial_grads.astype(jnp.bfloat16), 'dp').astype(jnp.float32)]
    all_to_all x4 -> x0, starting transfers between devices: 40.1 us -> none  [the longest x1 11.8 us: on_device(): lax.all_to_all(requests, 'table', split_axis=0, concat_axis=0, tiled=True)]
    gather x2 -> x0, local copies, waits for them, and re-layouts: 36.2 us -> none  [the longest x1 24 us: on_device(): jnp.take(table_half, jnp.minimum(asked_rows, row_count - 1), axis=0)]
    scatter x2 -> x0, local copies, waits for them, and re-layouts: 28.5 us -> none  [the longest x1 16.1 us: on_device(): jnp.full((slot_count,), row_count, jnp.int32).at[position].set(local_flat)]
    another operation x2 -> x0, other arithmetic: 18.6 us -> none
  transfers between devices with their start and end apart: 5 -> 0, of which waited for: 4 -> 0; matrix products, arithmetic and copies ran while one was open for 11% -> 0% of each run, Pallas kernels for 0% -> 0%
where the time goes in v3:
time: 133 us
  Pallas kernels  122 us (92%)
  local copies, waits for them, and re-layouts  5.89 us (4%)
  other arithmetic  3.23 us (2%)
    pallas_call x1, Pallas kernels, on_device(): pl.pallas_call(step_kernel, out_shape=(jax.ShapeDtypeStruct((bags, width)...  122 us
    unnamed x8, local copies, waits for them, and re-layouts  5.89 us

profile of v3, /device:TPU:32, one launch (start us, length us, event | category | flops | bytes accessed | tf_op | source)
XLA Modules:
  0.0 133.0 jit_solution(1565567132599235994)
XLA Ops:
  0.7 1.4 %fusion.12.slot_ref = s32[32,128]{1,0:T(8,128)} fusion(s32[4096]{0:T(1024)} %param.13, s32[]{:T(128)S(6)} %axis_index.12), kind=kLoop, calls=%fused_computation.37 | loop fusion | flops 352256 | bytes 32772 | tf_op jit(solution)/shard_map/reshape | solution.py:456
  2.0 0.9 compare_reduce_fusion
  3.0 0.9 fusion.3
  3.9 0.9 fusion.2.code_ref
  4.8 122.3 %step.1 = (bf16[512,128]{1,0:T(8,128)(2,1)}, f32[4096,128]{1,0:T(8,128)}, f32[32,128]{1,0:T(8,128)}, f32[128,128]{1,0:T(8,128)}) custom-call(s32[8,8,512]{2,1,0:T(8,128)} %fusion.2.code_ref, bf16[512,128]{1,0:T(8,128)(2,1)} %grads_ref.1, f32[4096,128]{1,0:T(8,128)} %table_ref.1, f32[32,128]{1,0:T(8,128)} %bitcast.11, s32[32,128]{1,0:T(8,128)} %fusion.12.slot_ref, ...), custom_call_target="tpu_custom_call" | custom-call | tf_op jit(solution)/shard_map/step/pallas_call | solution.py:397
  127.1 1.6 %copy.15 = bf16[512,128]{1,0:T(8,128)(2,1)} copy(bf16[512,128]{1,0:T(8,128)(2,1)} %get-tuple-element.16) | data formatting | bytes 262144
  128.6 0.0 copy-start.1
  128.7 0.0 copy-start
  128.7 3.1 %copy.16 = f32[4096,128]{1,0:T(8,128)} copy(f32[4096,128]{1,0:T(8,128)} %get-tuple-element.17) | data formatting | bytes 4194304
  131.7 0.0 copy-done.1
  131.7 0.6 copy.17
  132.3 0.0 copy-done
  132.3 0.6 copy.18
  (1 shorter events, 0.0 us)
Async XLA Ops:
  128.6 3.1 %copy-start.1 = (f32[32,128]{1,0:T(8,128)S(1)}, f32[32,128]{1,0:T(8,128)}, u32[]{:S(2)}) copy-start(f32[32,128]{1,0:T(8,128)} %get-tuple-element.10) | copy-start | bytes 49156
  128.7 3.7 %copy-start = (f32[128,128]{1,0:T(8,128)S(1)}, f32[128,128]{1,0:T(8,128)}, u32[]{:S(2)}) copy-start(f32[128,128]{1,0:T(8,128)} %get-tuple-element.19) | copy-start | bytes 196612

commit v4 on v3

--- a/solution.py
+++ b/solution.py
@@ -14,6 +14,7 @@
 NQ = NY * NC
 CAP = 128
 HALVES = 2
+PIECES = 2
 
 
 def near(k):
@@ -55,23 +56,23 @@
         return remote(code_ref.at[peer], code_in.at[place], code_s.at[peer], code_r.at[place],
                       table=on_line(peer))
 
-    def line_copy(peer, place):
-        return remote(grads_ref, line_in.at[place], line_s.at[peer], line_r.at[place],
-                      table=on_line(peer))
-
-    def g_copy(peer, place, s):
-        return remote(g_out.at[peer, s], g_in.at[place, s], g_s.at[peer, s], g_r.at[place, s],
-                      table=on_plane(peer))
-
-    def q_rows(o):
-        return pl.ds(pl.multiple_of(o * NZ, NZ), NZ)
-
-    def q_copy(peer, place):
-        return remote(q_out.at[q_rows(peer)], q_in.at[q_rows(place)], q_s.at[peer], q_r.at[place],
-                      table=on_plane(peer))
+    piece = bags // PIECES
+
+    def line_copy(way, hop, origin, i):
+        block = line_in.at[origin, pl.ds(i * piece, piece)]
+        return remote(block, block, line_s.at[way, hop, i], line_r.at[origin, i],
+                      table=on_line((z + 1 + way * (NZ - 2)) % NZ))
 
     def r_rows(o):
         return pl.ds(pl.multiple_of(o * CAP, CAP), CAP)
+
+    def g_copy(peer, place, s):
+        return remote(g_out.at[s, r_rows(peer)], g_in.at[s, r_rows(place)], g_s.at[peer, s],
+                      g_r.at[place, s], table=on_plane(peer))
+
+    def q_copy(peer, place, s):
+        return remote(q_out.at[s, peer], q_in.at[s, place], q_s.at[peer, s], q_r.at[place, s],
+                      table=on_plane(peer))
 
     def r_copy(peer, place, s):
         return remote(r_out.at[peer, s], r_in.at[s, r_rows(place)], r_s.at[peer, s],
@@ -135,47 +136,98 @@
 
     for peer in line_peers:
         code_copy(peer, z).start()
-    for peer in line_peers:
-        line_copy(peer, z).start()
+    line_in[z] = grads_ref[...]
+    for i in range(PIECES):
+        for way in (0, 1):
+            line_copy(way, 0, z, i).start()
     code_in[z] = code_ref[z]
-    line_in[z] = grads_ref[...]
 
     slot = lax.broadcasted_iota(I32, (CAP, bags), 0)
 
-    def pack(i, carry):
+    def pack(i):
         s = (z + NZ - near(i)) % NZ
 
         @pl.when(i > 0)
         def _():
             code_copy(s, s).wait_recv()
-            line_copy(s, s).wait_recv()
-
-        grads = line_in[s]
-        for k in range(1, NQ + 1):
-            o = (q + k) % NQ
-            code = code_in[s, pl.ds(o, 1), :]
+
+        for o in range(NQ):
+            code = code_in[s, o : o + 1, :]
             hot = slot == jnp.where(code < 0, -1, code & (CAP - 1))
-            mark = hot.astype(F32).astype(BF16)
-            marks[s, r_rows(o), :] = mark
-            lines = jnp.dot(mark, grads, preferred_element_type=F32).astype(BF16)
+            marks[s, o * CAP : (o + 1) * CAP, :] = hot.astype(F32).astype(BF16)
             named = jnp.where(hot, (code >> 7) + 1, 0)
             named = sum(named[:, b : b + CAP] for b in range(0, bags, CAP))
             named = jnp.sum(named.T, axis=0, keepdims=True)
-            named = jnp.where(named == 0, rows, named - 1)
-            if k < NQ:
-                q_out[pl.ds(o * NZ + s, 1), :] = named
-                g_out[o, s] = lines
-                g_copy(o, q, s).start()
-            else:
-                q_in[pl.ds(o * NZ + s, 1), :] = named
-                g_in[o, s] = lines
-        return carry
-
-    lax.fori_loop(0, NZ, pack, 0)
-    for peer in plane_peers:
-        q_copy(peer, q).start()
-    for peer in plane_peers:
-        q_copy(peer, peer).wait_recv()
+            q_out[s, o] = jnp.where(named == 0, rows, named - 1)
+        for peer in plane_peers:
+            q_copy(peer, q, s).start()
+        q_in[s, q] = q_out[s, q]
+        g_out[s] = jnp.dot(marks[s], line_in[s], preferred_element_type=F32).astype(BF16)
+        for peer in plane_peers:
+            g_copy(peer, q, s).start()
+        g_in[s, r_rows(q), :] = g_out[s, r_rows(q), :]
+
+    def pass_on(h):
+        for i in range(PIECES):
+            for way, last in ((0, NZ // 2), (1, NZ // 2 - 1)):
+                origin = (z + NZ - h + way * 2 * h) % NZ
+
+                @pl.when(h <= last)
+                def _():
+                    line_copy(way, 0, origin, i).wait_recv()
+
+                @pl.when(h < last)
+                def _():
+                    line_copy(way, h, origin, i).start()
+
+    chunk = 256
+    low_row = lax.broadcasted_iota(I32, (chunk, CAP), 0)
+
+    def add(i):
+        s = (z + NZ - near(i)) % NZ
+        for k in range(1, NQ):
+            o = (q + k) % NQ
+            q_copy(o, o, s).wait_recv()
+            g_copy(o, o, s).wait_recv()
+        names = [q_in[s, o] for o in range(NQ)]
+        high = (jnp.concatenate(names, axis=0) // quarter).T
+        grads = []
+        for o in range(NQ):
+            block = jnp.broadcast_to(high[:, o : o + 1], (CAP, width))
+            lines = g_in[s, o * CAP : (o + 1) * CAP, :]
+            grads.append(
+                jnp.concatenate([(block == d).astype(F32).astype(BF16) * lines for d in range(dp)], axis=1)
+            )
+        grads = jnp.concatenate(grads, axis=0)
+        low = [one & (quarter - 1) for one in names]
+        for b in range(0, quarter, chunk):
+            hot = jnp.concatenate(
+                [(low_row == one - b).astype(F32).astype(BF16) for one in low], axis=1
+            )
+            total[b : b + chunk, :] += jnp.dot(hot, grads, preferred_element_type=F32)
+
+    def relay(p, carry):
+        def packs(i, carry):
+            pl.when(jnp.logical_and(i >= 0, i < NZ))(lambda: pack(i))
+            return carry
+
+        def adds(i, carry):
+            pl.when(i >= 0)(lambda: add(i))
+            return carry
+
+        lax.fori_loop(2 * p - 1, 2 * p + 1, packs, 0)
+        pass_on(p + 1)
+        lax.fori_loop(2 * p - 3, 2 * p - 1, adds, 0)
+        return carry
+
+    lax.fori_loop(0, NZ // 2 + 1, relay, 0)
+    add(NZ - 1)
+    for h in range(HALVES):
+        for d in range(dp):
+            part[d, half_rows(h), :] = total[half_rows(h), d * width : (d + 1) * width].astype(BF16)
+        for peer in dp_peers:
+            part_copy(peer, mine, h).start()
+
     fetch = pltpu.make_async_copy(q_in, q_smem, smem_sem)
     fetch.start()
     fetch.wait()
@@ -183,7 +235,7 @@
 
     def pick(o, s):
         for i in range(CAP):
-            line[pl.ds(i, 1), :] = table[pl.ds(q_smem[o * NZ + s, i], 1), :]
+            line[pl.ds(i, 1), :] = table[pl.ds(q_smem[s, o, 0, i], 1), :]
         return line[...].astype(BF16)
 
     def serve(i, carry):
@@ -204,41 +256,6 @@
         return carry
 
     lax.fori_loop(0, NZ * NQ, serve, 0)
-
-    chunk = 256
-    low_row = lax.broadcasted_iota(I32, (chunk, CAP), 0)
-
-    def add(k, carry):
-        o = (q + NQ - k) % NQ
-
-        @pl.when(k > 0)
-        def _():
-            for s in range(NZ):
-                g_copy(o, o, s).wait_recv()
-
-        names = q_in[q_rows(o), :]
-        low = names & (quarter - 1)
-        high = (names // quarter).T
-        grads = []
-        for s in range(NZ):
-            block = jnp.broadcast_to(high[:, s : s + 1], (CAP, width))
-            mine_only = [(block == d).astype(F32).astype(BF16) * g_in[o, s] for d in range(dp)]
-            grads.append(jnp.concatenate(mine_only, axis=1))
-        grads = jnp.concatenate(grads, axis=0)
-        for b in range(0, quarter, chunk):
-            hot = jnp.concatenate(
-                [(low_row == low[s : s + 1, :] - b).astype(F32).astype(BF16) for s in range(NZ)],
-                axis=1,
-            )
-            total[b : b + chunk, :] += jnp.dot(hot, grads, preferred_element_type=F32)
-        return carry
-
-    lax.fori_loop(0, NQ, add, 0)
-    for h in range(HALVES):
-        for d in range(dp):
-            part[d, half_rows(h), :] = total[half_rows(h), d * width : (d + 1) * width].astype(BF16)
-        for peer in dp_peers:
-            part_copy(peer, mine, h).start()
 
     def pool(i, carry):
         s = (z + near(NZ - 1 - i)) % NZ
@@ -260,8 +277,6 @@
         sums[mine, half_rows(h), :] = summed.astype(BF16)
         for peer in dp_peers:
             sum_copy(peer, mine, h).start()
-
-    lax.fori_loop(0, 4, pool, 0)
 
     slots = placed.shape[0]
     place_chunk = 256
@@ -286,6 +301,7 @@
 
     for h in range(HALVES):
         update(mine, h)
+    lax.fori_loop(0, 4, pool, 0)
     for h in range(HALVES):
         for peer in dp_peers:
             sum_copy(peer, peer, h).wait_recv()
@@ -347,16 +363,21 @@
     core_copy().wait_send()
     for peer in line_peers:
         code_copy(peer, z).wait_send()
-        line_copy(peer, z).wait_send()
         pool_copy(peer, z).wait_send()
         z_copy(peer, z).wait_send()
+
+    for i in range(PIECES):
+        for hop in range(NZ // 2):
+            line_copy(0, hop, z, i).wait_send()
+        for hop in range(NZ // 2 - 1):
+            line_copy(1, hop, z, i).wait_send()
 
     def sent(k, carry):
         peer = (q + k) % NQ
         for s in range(NZ):
             g_copy(peer, q, s).wait_send()
             r_copy(peer, q, s).wait_send()
-        q_copy(peer, q).wait_send()
+            q_copy(peer, q, s).wait_send()
         return carry
 
     lax.fori_loop(1, NQ, sent, 0)
@@ -410,11 +431,11 @@
             pltpu.VMEM((NZ, bags, width), BF16),
             pltpu.VMEM((NZ, NQ, bags), I32),
             pltpu.VMEM((NZ, NQ * CAP, bags), BF16),
-            pltpu.VMEM((NQ, NZ, CAP, width), BF16),
-            pltpu.VMEM((NQ, NZ, CAP, width), BF16),
-            pltpu.VMEM((NQ * NZ, CAP), I32),
-            pltpu.VMEM((NQ * NZ, CAP), I32),
-            pltpu.SMEM((NQ * NZ, CAP), I32),
+            pltpu.VMEM((NZ, NQ * CAP, width), BF16),
+            pltpu.VMEM((NZ, NQ * CAP, width), BF16),
+            pltpu.VMEM((NZ, NQ, 1, CAP), I32),
+            pltpu.VMEM((NZ, NQ, 1, CAP), I32),
+            pltpu.SMEM((NZ, NQ, 1, CAP), I32),
             pltpu.VMEM((NQ, NZ, CAP, width), BF16),
             pltpu.VMEM((NZ, NQ * CAP, width), BF16),
             pltpu.VMEM((quarter, dp * width), F32),
@@ -433,10 +454,9 @@
             pltpu.VMEM((2 * NY, share, width), F32),
             pltpu.VMEM((dp, share, width), F32),
         ]
-        + [dma((NZ,))] * 4
-        + [dma((NQ, NZ))] * 2
-        + [dma((NQ,))] * 2
-        + [dma((NQ, NZ))] * 2
+        + [dma((NZ,))] * 2
+        + [dma((2, NZ // 2, PIECES)), dma((NZ, PIECES))]
+        + [dma((NQ, NZ))] * 6
         + [dma((dp, HALVES))] * 4
         + [dma((NZ,))] * 2
         + [dma] * 2

time: 133 us -> 111 us (0.83)
  Pallas kernels: 122 us -> 100 us
    pallas_call x1, Pallas kernels: 122 us -> 100 us  [on_device(): pl.pallas_call(step_kernel, out_shape=(jax.ShapeDtypeStruct((bags, width)...]
where the time goes in v4:
time: 111 us
  Pallas kernels  100 us (90%)
  local copies, waits for them, and re-layouts  5.89 us (5%)
  other arithmetic  3.23 us (3%)
    pallas_call x1, Pallas kernels, on_device(): pl.pallas_call(step_kernel, out_shape=(jax.ShapeDtypeStruct((bags, width)...  100 us
    unnamed x8, local copies, waits for them, and re-layouts  5.89 us

profile of v4, /device:TPU:32, one launch (start us, length us, event | category | flops | bytes accessed | tf_op | source)
XLA Modules:
  0.0 110.9 jit_solution(13906994786118338811)
XLA Ops:
  0.7 1.4 %fusion.12.slot_ref = s32[32,128]{1,0:T(8,128)} fusion(s32[4096]{0:T(1024)} %param.13, s32[]{:T(128)S(6)} %axis_index.12), kind=kLoop, calls=%fused_computation.37 | loop fusion | flops 352256 | bytes 32772 | tf_op jit(solution)/shard_map/reshape | solution.py:476
  2.0 0.9 compare_reduce_fusion
  3.0 0.9 fusion.3
  3.9 0.9 fusion.2.code_ref
  4.8 100.2 %step.1 = (bf16[512,128]{1,0:T(8,128)(2,1)}, f32[4096,128]{1,0:T(8,128)}, f32[32,128]{1,0:T(8,128)}, f32[128,128]{1,0:T(8,128)}) custom-call(s32[8,8,512]{2,1,0:T(8,128)} %fusion.2.code_ref, bf16[512,128]{1,0:T(8,128)(2,1)} %grads_ref.1, f32[4096,128]{1,0:T(8,128)} %table_ref.1, f32[32,128]{1,0:T(8,128)} %bitcast.11, s32[32,128]{1,0:T(8,128)} %fusion.12.slot_ref, ...), custom_call_target="tpu_custom_call" | custom-call | tf_op jit(solution)/shard_map/step/pallas_call | solution.py:418
  105.0 1.6 %copy.15 = bf16[512,128]{1,0:T(8,128)(2,1)} copy(bf16[512,128]{1,0:T(8,128)(2,1)} %get-tuple-element.16) | data formatting | bytes 262144
  106.5 0.0 copy-start.1
  106.5 0.0 copy-start
  106.5 3.1 %copy.16 = f32[4096,128]{1,0:T(8,128)} copy(f32[4096,128]{1,0:T(8,128)} %get-tuple-element.17) | data formatting | bytes 4194304
  109.6 0.0 copy-done.1
  109.6 0.6 copy.17
  110.2 0.0 copy-done
  110.2 0.6 copy.18
  (1 shorter events, 0.0 us)
Async XLA Ops:
  106.5 3.1 %copy-start.1 = (f32[32,128]{1,0:T(8,128)S(1)}, f32[32,128]{1,0:T(8,128)}, u32[]{:S(2)}) copy-start(f32[32,128]{1,0:T(8,128)} %get-tuple-element.10) | copy-start | bytes 49156
  106.5 3.7 %copy-start = (f32[128,128]{1,0:T(8,128)S(1)}, f32[128,128]{1,0:T(8,128)}, u32[]{:S(2)}) copy-start(f32[128,128]{1,0:T(8,128)} %get-tuple-element.19) | copy-start | bytes 196612

commit v5 on v4

--- a/solution.py
+++ b/solution.py
@@ -8,6 +8,7 @@
 LEARN = 0.5
 EPSILON = 1e-06
 F32, BF16, I32 = jnp.float32, jnp.bfloat16, jnp.int32
+ANY = pl.BlockSpec(memory_space=pl.ANY)
 VMEM = pl.BlockSpec(memory_space=pltpu.VMEM)
 MESH = pl.DeviceIdType.MESH
 NY, NZ, NC = 4, 8, 2
@@ -23,13 +24,13 @@
 
 
 def step_kernel(
-    code_ref, grads_ref, table_ref, accum_ref, slot_ref, parity_ref,
-    pooled_ref, new_table_ref, new_accum_ref, new_parity_ref,
-    table, wide_accum, line_in, code_in, marks, g_out, g_in, q_out, q_in, q_smem, r_out, r_in,
+    code_ref, grads_ref, table_ref, accum_ref, home_ref,
+    pooled_ref, fresh_ref, new_accum_ref, change_ref,
+    slot_ref, table, wide_accum, line_in, code_in, marks, g_out, g_in, q_out, q_in, q_smem, r_out, r_in,
     total, part, quarter_in, sums, pool_out, pool_in, line, placed, core_out, core_in,
-    z_out, z_in, y_out, y_in, x_part,
+    z_out, z_in, z_sums, y_out, y_in, x_part,
     code_s, code_r, line_s, line_r, g_s, g_r, q_s, q_r, r_s, r_r, part_s, part_r, sum_s, sum_r,
-    pool_s, pool_r, core_s, core_r, z_s, z_r, y_s, y_r, x_s, x_r, table_sem, smem_sem,
+    pool_s, pool_r, core_s, core_r, z_s, z_r, y_s, y_r, x_s, x_r, table_sem, smem_sem, fresh, fresh_sem,
 ):
     bags = code_ref.shape[2]
     rows, width = table_ref.shape
@@ -67,16 +68,31 @@
         return pl.ds(pl.multiple_of(o * CAP, CAP), CAP)
 
     def g_copy(peer, place, s):
-        return remote(g_out.at[s, r_rows(peer)], g_in.at[s, r_rows(place)], g_s.at[peer, s],
-                      g_r.at[place, s], table=on_plane(peer))
+        return remote(g_out.at[s, r_rows(peer)], g_in.at[s, r_rows(place)], g_s.at[s],
+                      g_r.at[s], table=on_plane(peer))
 
     def q_copy(peer, place, s):
-        return remote(q_out.at[s, peer], q_in.at[s, place], q_s.at[peer, s], q_r.at[place, s],
+        return remote(q_out.at[s, peer], q_in.at[s, place], q_s.at[s], q_r.at[s],
                       table=on_plane(peer))
 
     def r_copy(peer, place, s):
-        return remote(r_out.at[peer, s], r_in.at[s, r_rows(place)], r_s.at[peer, s],
-                      r_r.at[place, s], table=on_plane(peer))
+        return remote(r_out.at[s, r_rows(peer)], r_in.at[s, r_rows(place)], r_s.at[s],
+                      r_r.at[s], table=on_plane(peer))
+
+    others = pl.ds(0, NQ - 1)
+    other_rows = pl.ds(0, (NQ - 1) * CAP)
+
+    def all_g(s):
+        return remote(g_out.at[s, other_rows], g_in.at[s, other_rows], g_s.at[s], g_r.at[s],
+                      table=on_plane((q + 1) % NQ))
+
+    def all_q(s):
+        return remote(q_out.at[s, others], q_in.at[s, others], q_s.at[s], q_r.at[s],
+                      table=on_plane((q + 1) % NQ))
+
+    def all_r(s):
+        return remote(r_out.at[s, other_rows], r_in.at[s, other_rows], r_s.at[s], r_r.at[s],
+                      table=on_plane((q + 1) % NQ))
 
     def half_rows(h):
         return pl.ds(h * half, half)
@@ -111,6 +127,7 @@
     line_from = [(z + NZ - near(k)) % NZ for k in range(1, NZ)]
     plane_peers = [(q + k) % NQ for k in range(1, NQ)]
     dp_peers = [(mine + k) % dp for k in (1, 3, 2)]
+    right, left, far = [(mine + k) % dp for k in (1, dp - 1, 2)]
     y_peers = [(y + k) % NY for k in (1, 3, 2)]
 
     load = pltpu.make_async_copy(table_ref, table.at[0:rows], table_sem)
@@ -122,24 +139,14 @@
         pl.semaphore_signal(barrier, inc=1, device_id={"table": on_plane(peer)}, device_id_type=MESH)
     for peer in dp_peers:
         pl.semaphore_signal(barrier, inc=1, device_id={"dp": peer}, device_id_type=MESH)
-    table[rows : rows + 8, :] = jnp.zeros((8, width), F32)
-    total[...] = jnp.zeros_like(total)
-    placed[...] = jnp.zeros_like(placed)
-
-    def widen(i, carry):
-        block = jnp.broadcast_to(accum_ref[pl.ds(i, 1), :], (128, 128))
-        wide_accum[pl.ds(pl.multiple_of(i * 128, 128), 128), :] = block.T
-        return carry
-
-    lax.fori_loop(0, rows // 128, widen, 0)
+
     pl.semaphore_wait(barrier, len(line_peers) + len(plane_peers) + len(dp_peers))
-
-    for peer in line_peers:
-        code_copy(peer, z).start()
     line_in[z] = grads_ref[...]
     for i in range(PIECES):
         for way in (0, 1):
             line_copy(way, 0, z, i).start()
+    for peer in line_peers:
+        code_copy(peer, z).start()
     code_in[z] = code_ref[z]
 
     slot = lax.broadcasted_iota(I32, (CAP, bags), 0)
@@ -185,10 +192,8 @@
 
     def add(i):
         s = (z + NZ - near(i)) % NZ
-        for k in range(1, NQ):
-            o = (q + k) % NQ
-            q_copy(o, o, s).wait_recv()
-            g_copy(o, o, s).wait_recv()
+        all_q(s).wait_recv()
+        all_g(s).wait_recv()
         names = [q_in[s, o] for o in range(NQ)]
         high = (jnp.concatenate(names, axis=0) // quarter).T
         grads = []
@@ -206,28 +211,51 @@
             )
             total[b : b + chunk, :] += jnp.dot(hot, grads, preferred_element_type=F32)
 
+    share = change_ref.shape[0] // dp
+
+    def prepare():
+        count = change_ref.shape[0]
+        home = home_ref[...]
+        holder, place = home // count, home % count
+        order = (holder % NC * NY + holder // (NZ * NC)) * NZ + holder // NC % NZ
+        slot_ref[...] = jnp.where(place // share == mine, order * share + place % share, -1)
+
+        table[rows : rows + 8, :] = jnp.zeros((8, width), F32)
+        total[...] = jnp.zeros_like(total)
+        placed[...] = jnp.zeros_like(placed)
+
+        def widen(i, carry):
+            block = jnp.broadcast_to(accum_ref[pl.ds(i, 1), :], (128, 128))
+            wide_accum[pl.ds(pl.multiple_of(i * 128, 128), 128), :] = block.T
+            return carry
+
+        lax.fori_loop(0, rows // 128, widen, 0)
+
     def relay(p, carry):
         def packs(i, carry):
             pl.when(jnp.logical_and(i >= 0, i < NZ))(lambda: pack(i))
             return carry
 
         def adds(i, carry):
-            pl.when(i >= 0)(lambda: add(i))
+            add(i)
             return carry
 
         lax.fori_loop(2 * p - 1, 2 * p + 1, packs, 0)
+        pl.when(p == 0)(prepare)
         pass_on(p + 1)
-        lax.fori_loop(2 * p - 3, 2 * p - 1, adds, 0)
+        lax.fori_loop(jnp.maximum(2 * p - 3, 0), jnp.maximum(2 * p - 1, 0), adds, 0)
         return carry
 
     lax.fori_loop(0, NZ // 2 + 1, relay, 0)
-    add(NZ - 1)
-    for h in range(HALVES):
+    lax.fori_loop(NZ - 1, NZ, lambda i, carry: (add(i), carry)[1], 0)
+    def part_start(h):
         for d in range(dp):
             part[d, half_rows(h), :] = total[half_rows(h), d * width : (d + 1) * width].astype(BF16)
         for peer in dp_peers:
             part_copy(peer, mine, h).start()
 
+    part_start(0)
+
     fetch = pltpu.make_async_copy(q_in, q_smem, smem_sem)
     fetch.start()
     fetch.wait()
@@ -238,30 +266,21 @@
             line[pl.ds(i, 1), :] = table[pl.ds(q_smem[s, o, 0, i], 1), :]
         return line[...].astype(BF16)
 
-    def serve(i, carry):
-        s = (z + near(NZ - 1 - i // NQ)) % NZ
-        k = i % NQ
-        o = (q + k) % NQ
-        picked = pick(o, s)
-
-        @pl.when(k == 0)
-        def _():
-            r_in[s, r_rows(o), :] = picked
-
-        @pl.when(k > 0)
-        def _():
-            r_out[o, s] = picked
+    def serve(j):
+        s = (z + near(NZ - 1 - j)) % NZ
+
+        def one(k, carry):
+            o = (q + k) % NQ
+            r_out[s, r_rows(o), :] = pick(o, s)
             r_copy(o, q, s).start()
-
-        return carry
-
-    lax.fori_loop(0, NZ * NQ, serve, 0)
+            return carry
+
+        lax.fori_loop(1, NQ, one, 0)
+        r_in[s, r_rows(q), :] = pick(q, s)
 
     def pool(i, carry):
         s = (z + near(NZ - 1 - i)) % NZ
-        for k in range(1, NQ):
-            o = (q + k) % NQ
-            r_copy(o, o, s).wait_recv()
+        all_r(s).wait_recv()
         pooled = lax.dot_general(
             r_in[s], marks[s], (((0,), (0,)), ((), ())), preferred_element_type=F32
         )
@@ -269,18 +288,39 @@
         pool_copy(s, z).start()
         return carry
 
-    for h in range(HALVES):
+
+    def dp_sum(h):
         summed = part[mine, half_rows(h), :].astype(F32)
         for peer in dp_peers:
             part_copy(peer, peer, h).wait_recv()
             summed = summed + quarter_in[peer, half_rows(h), :].astype(F32)
         sums[mine, half_rows(h), :] = summed.astype(BF16)
-        for peer in dp_peers:
+        for peer in (right, left):
             sum_copy(peer, mine, h).start()
+
+    def serves(j, carry):
+        serve(j)
+
+        @pl.when(j >= 4)
+        def _():
+            pool(j - 4, 0)
+
+        return carry
+
+    lax.fori_loop(0, 4, serves, 0)
+    part_start(1)
+    lax.fori_loop(4, 5, serves, 0)
+    dp_sum(0)
+    lax.fori_loop(5, NZ, serves, 0)
+    dp_sum(1)
 
     slots = placed.shape[0]
     place_chunk = 256
     place_row = lax.broadcasted_iota(I32, (place_chunk, 128), 0)
+
+    def fresh_copy(d, h):
+        there = pl.ds(pl.multiple_of(d * quarter + h * half, half), half)
+        return pltpu.make_async_copy(fresh.at[there], fresh_ref.at[there], fresh_sem.at[d, h])
 
     def update(d, h):
         base = pl.multiple_of(d * quarter + h * half, half)
@@ -290,7 +330,8 @@
         accum = wide_accum[there, :] + squares
         wide_accum[there, :] = accum
         delta = g * (-LEARN) * lax.rsqrt(accum + EPSILON)
-        new_table_ref[there, :] = table[there, :] + delta
+        fresh[there, :] = table[there, :] + delta
+        fresh_copy(d, h).start()
         delta = delta.astype(BF16)
         lines = [slot_ref[pl.ds(base // 128 + i, 1), :] for i in range(half // 128)]
         for b in range(0, slots, place_chunk):
@@ -299,13 +340,27 @@
             )
             placed[b : b + place_chunk, :] += jnp.dot(hot, delta, preferred_element_type=F32)
 
-    for h in range(HALVES):
-        update(mine, h)
-    lax.fori_loop(0, 4, pool, 0)
-    for h in range(HALVES):
-        for peer in dp_peers:
-            sum_copy(peer, peer, h).wait_recv()
-            update(peer, h)
+    def pass_sum(origin, peer, h):
+        block = sums.at[origin, half_rows(h)]
+        return remote(block, block, sum_s.at[far, h], sum_r.at[origin, h], dp=peer)
+
+    def arrived(d, h):
+        sum_copy(d, d, h).wait_recv()
+        if d is left and h == 0:
+            pass_sum(left, right, 0).start()
+        if d is right and h == 1:
+            pass_sum(right, left, 1).start()
+        update(d, h)
+
+    update(mine, 0)
+    arrived(left, 0)
+    arrived(right, 0)
+    update(mine, 1)
+    arrived(right, 1)
+    arrived(left, 1)
+    lax.fori_loop(4, 6, pool, 0)
+    arrived(far, 0)
+    arrived(far, 1)
 
     per_core = slots // NC
     core_out[...] = placed[pl.ds(pl.multiple_of((1 - c) * per_core, per_core), per_core), :].astype(BF16)
@@ -313,52 +368,48 @@
     kept = pl.ds(pl.multiple_of(c * per_core, per_core), per_core)
     core_copy().wait_recv()
     placed[kept, :] = placed[kept, :] + core_in[...].astype(F32)
-    per_z = per_core // NZ
+    per_y = per_core // NY
+    for peer in y_peers:
+        begin = pl.multiple_of(c * per_core + peer * per_y, per_y)
+        y_out[peer] = placed[pl.ds(begin, per_y), :].astype(BF16)
+        y_copy(peer, y).start()
+    y_sum = placed[pl.ds(pl.multiple_of(c * per_core + y * per_y, per_y), per_y), :]
+    lax.fori_loop(6, NZ - 1, pool, 0)
+    for peer in y_peers:
+        y_copy(peer, peer).wait_recv()
+        y_sum = y_sum + y_in[peer].astype(F32)
+    for k in range(NZ):
+        z_sums[k] = y_sum[k * share : (k + 1) * share, :]
     for peer in line_peers:
-        begin = pl.multiple_of(c * per_core + peer * per_z, per_z)
-        z_out[peer] = placed[pl.ds(begin, per_z), :].astype(BF16)
+        z_out[peer] = z_sums[peer].astype(BF16)
         z_copy(peer, z).start()
-    z_sum = placed[pl.ds(pl.multiple_of(c * per_core + z * per_z, per_z), per_z), :]
-    lax.fori_loop(4, NZ - 1, pool, 0)
-    for k in range(1, NQ):
-        o = (q + k) % NQ
-        r_copy(o, o, z).wait_recv()
+    all_r(z).wait_recv()
     own_pool = lax.dot_general(
         r_in[z], marks[z], (((0,), (0,)), ((), ())), preferred_element_type=F32
     )
+
+    def narrow(i, carry):
+        block = wide_accum[pl.ds(pl.multiple_of(i * 128, 128), 128), :]
+        new_accum_ref[pl.ds(i, 1), :] = block.T[0:1, :]
+        return carry
+
+    lax.fori_loop(0, rows // 128, narrow, 0)
+    z_sum = z_sums[z]
     for peer in line_from:
         z_copy(peer, peer).wait_recv()
         z_sum = z_sum + z_in[peer].astype(F32)
-    per_y = per_z // NY
-    for j in range(NY):
-        y_in[NY + j] = z_sum[j * per_y : (j + 1) * per_y, :]
-    for peer in y_peers:
-        y_out[peer] = y_in[NY + peer]
-        y_copy(peer, y).start()
-    y_sum = y_in[NY + y]
-    for peer in y_peers:
-        y_copy(peer, peer).wait_recv()
-        y_sum = y_sum + y_in[peer]
-    x_part[mine] = y_sum
+    x_part[mine] = z_sum
     for peer in dp_peers:
         x_copy(peer, mine).start()
-
     for peer in line_from:
         pool_copy(peer, peer).wait_recv()
         own_pool = own_pool + pool_in[peer].astype(F32)
     pooled_ref[...] = own_pool.T.astype(BF16)
-
-    def narrow(i, carry):
-        block = wide_accum[pl.ds(pl.multiple_of(i * 128, 128), 128), :]
-        new_accum_ref[pl.ds(i, 1), :] = block.T[0:1, :]
-        return carry
-
-    lax.fori_loop(0, rows // 128, narrow, 0)
     for peer in dp_peers:
         x_copy(peer, peer).wait_recv()
     for d in range(dp):
-        lines = slice(d * per_y, (d + 1) * per_y)
-        new_parity_ref[lines, :] = parity_ref[lines, :] + x_part[d]
+        lines = slice(d * share, (d + 1) * share)
+        change_ref[lines, :] = x_part[d]
 
     core_copy().wait_send()
     for peer in line_peers:
@@ -372,30 +423,36 @@
         for hop in range(NZ // 2 - 1):
             line_copy(1, hop, z, i).wait_send()
 
-    def sent(k, carry):
-        peer = (q + k) % NQ
-        for s in range(NZ):
-            g_copy(peer, q, s).wait_send()
-            r_copy(peer, q, s).wait_send()
-            q_copy(peer, q, s).wait_send()
-        return carry
-
-    lax.fori_loop(1, NQ, sent, 0)
+    for k in range(NZ):
+        all_g(k).wait_send()
+        all_q(k).wait_send()
+        all_r(k).wait_send()
     for peer in dp_peers:
         for h in range(HALVES):
             part_copy(peer, mine, h).wait_send()
+        x_copy(peer, mine).wait_send()
+    for h in range(HALVES):
+        for peer in (right, left):
             sum_copy(peer, mine, h).wait_send()
-        x_copy(peer, mine).wait_send()
+    pass_sum(left, right, 0).wait_send()
+    pass_sum(right, left, 1).wait_send()
     for peer in y_peers:
         y_copy(peer, y).wait_send()
+    for d in range(dp):
+        for h in range(HALVES):
+            fresh_copy(d, h).wait()
+
+
+def publish_kernel(pooled, fresh, accum, change, parity, *outs):
+    for one, out in zip((pooled, fresh, accum), outs):
+        out[...] = one[...]
+    outs[3][...] = parity[...] + change[...]
 
 
 def on_device(owners, local_rows, grad_pooled, table, accum, parity, parity_slot):
     table_count, dp = lax.axis_size("table"), lax.axis_size("dp")
     bags = owners.shape[0]
     rows, width = table.shape
-    mine = lax.axis_index("dp")
-
     index = jnp.arange(table_count, dtype=I32)
     owner_at = (index % NQ // NC * NZ + index // NQ) * NC + index % NC
     named = owners.T[:, None, :] == owner_at[None, :, None]
@@ -407,15 +464,10 @@
 
     count = parity.shape[0]
     share = count // dp
-    holder, place = parity_slot // count, parity_slot % count
-    holder_y, holder_z, holder_c = holder // (NZ * NC), holder // NC % NZ, holder % NC
-    order = (holder_c * NZ + holder_z) * NY + holder_y
-    slot = jnp.where(place // share == mine, order * share + place % share, -1)
     slots = table_count * share
-
     quarter = rows // dp
     dma = pltpu.SemaphoreType.DMA
-    pooled, new_table, new_accum, new_parity = pl.pallas_call(
+    pooled, fresh, new_accum, change = pl.pallas_call(
         step_kernel,
         out_shape=(
             jax.ShapeDtypeStruct((bags, width), BF16),
@@ -423,9 +475,10 @@
             jax.ShapeDtypeStruct((rows // 128, 128), F32),
             jax.ShapeDtypeStruct((count, width), F32),
         ),
-        in_specs=[VMEM, VMEM, pl.BlockSpec(memory_space=pl.ANY), VMEM, VMEM, VMEM],
-        out_specs=(VMEM,) * 4,
+        in_specs=[VMEM, VMEM, ANY, VMEM, VMEM],
+        out_specs=(VMEM, ANY, VMEM, VMEM),
         scratch_shapes=[
+            pltpu.VMEM((rows // 128, 128), I32),
             pltpu.VMEM((rows + 8, width), F32),
             pltpu.VMEM((rows, 128), F32),
             pltpu.VMEM((NZ, bags, width), BF16),
@@ -436,7 +489,7 @@
             pltpu.VMEM((NZ, NQ, 1, CAP), I32),
             pltpu.VMEM((NZ, NQ, 1, CAP), I32),
             pltpu.SMEM((NZ, NQ, 1, CAP), I32),
-            pltpu.VMEM((NQ, NZ, CAP, width), BF16),
+            pltpu.VMEM((NZ, NQ * CAP, width), BF16),
             pltpu.VMEM((NZ, NQ * CAP, width), BF16),
             pltpu.VMEM((quarter, dp * width), F32),
             pltpu.VMEM((dp, quarter, width), BF16),
@@ -448,22 +501,24 @@
             pltpu.VMEM((slots, width), F32),
             pltpu.VMEM((slots // NC, width), BF16),
             pltpu.VMEM((slots // NC, width), BF16),
-            pltpu.VMEM((NZ, NY * share, width), BF16),
-            pltpu.VMEM((NZ, NY * share, width), BF16),
-            pltpu.VMEM((NY, share, width), F32),
-            pltpu.VMEM((2 * NY, share, width), F32),
+            pltpu.VMEM((NZ, share, width), BF16),
+            pltpu.VMEM((NZ, share, width), BF16),
+            pltpu.VMEM((NZ, share, width), F32),
+            pltpu.VMEM((NY, NZ * share, width), BF16),
+            pltpu.VMEM((NY, NZ * share, width), BF16),
             pltpu.VMEM((dp, share, width), F32),
         ]
         + [dma((NZ,))] * 2
         + [dma((2, NZ // 2, PIECES)), dma((NZ, PIECES))]
-        + [dma((NQ, NZ))] * 6
+        + [dma((NZ,))] * 6
         + [dma((dp, HALVES))] * 4
         + [dma((NZ,))] * 2
         + [dma] * 2
         + [dma((NZ,))] * 2
         + [dma((NY,))] * 2
         + [dma((dp,))] * 2
-        + [dma, dma],
+        + [dma, dma]
+        + [pltpu.VMEM((rows, width), F32), dma((dp, HALVES))],
         compiler_params=pltpu.CompilerParams(
             vmem_limit_bytes=56 * 1024 * 1024, collective_id=0, has_side_effects=True
         ),
@@ -473,9 +528,20 @@
         grad_pooled,
         table,
         accum.reshape(rows // 128, 128),
-        slot.reshape(rows // 128, 128),
-        parity,
+        parity_slot.reshape(rows // 128, 128),
     )
+    def part(array):
+        return pl.BlockSpec((array.shape[0] // 4, array.shape[1]), lambda i: (i, 0))
+
+    results = (pooled, fresh, new_accum, change)
+    pooled, new_table, new_accum, new_parity = pl.pallas_call(
+        publish_kernel,
+        grid=(4,),
+        out_shape=tuple(jax.ShapeDtypeStruct(one.shape, one.dtype) for one in results),
+        in_specs=[part(one) for one in results + (parity,)],
+        out_specs=tuple(part(one) for one in results),
+        name="publish",
+    )(*results, parity)
     return (pooled, new_table, new_accum.reshape(rows), new_parity)
 
 

time: 111 us -> 92.6 us (0.83)
  Pallas kernels: 100 us -> 88.3 us
  local copies, waits for them, and re-layouts: 5.89 us -> 0 us
  other arithmetic: 3.23 us -> 1.85 us
    pallas_call x1, Pallas kernels: 100 us -> 84.5 us  [on_device(): pl.pallas_call(step_kernel, out_shape=(jax.ShapeDtypeStruct((bags, width)...]
    unnamed x8 -> x0, local copies, waits for them, and re-layouts: 5.89 us -> none
    pallas_call x0 -> x1, Pallas kernels: none -> 3.82 us  [on_device(): pl.pallas_call(publish_kernel, grid=(4,), out_shape=tuple((jax.ShapeDtype...]
    reshape x1 -> x0, other arithmetic: 1.39 us -> none  [on_device(): slot.reshape(rows // 128, 128)]
where the time goes in v5:
time: 92.6 us; the launch traced here: 91.8 us
  Pallas kernels  88.3 us (95%)
  other arithmetic  1.85 us (2%)
    pallas_call x1, Pallas kernels, on_device(): pl.pallas_call(step_kernel, out_shape=(jax.ShapeDtypeStruct((bags, width)...  84.5 us
    pallas_call x1, Pallas kernels, on_device(): pl.pallas_call(publish_kernel, grid=(4,), out_shape=tuple((jax.ShapeDtype...  3.82 us

profile of v5, /device:TPU:32, one launch (start us, length us, event | category | flops | bytes accessed | tf_op | source)
XLA Modules:
  0.0 91.8 jit_solution(10701717272334589113)
XLA Ops:
  0.6 0.9 %compare_reduce_fusion = pred[64,512]{1,0:T(8,128)(4,1)S(1)} fusion(s32[8,512]{1,0:T(8,128)} %bitcast.8, s32[64]{0:T(128)S(1)} %fusion.4), kind=kLoop, calls=%fused_computation.1 | loop fusion | flops 491520 | bytes 49408 | tf_op jit(solution)/shard_map/reduce_or | solution.py:459
  1.6 0.9 fusion.3
  2.5 0.9 fusion.2.code_ref
  3.4 84.5 %step.1 = (bf16[512,128]{1,0:T(8,128)(2,1)}, f32[4096,128]{1,0:T(8,128)}, f32[32,128]{1,0:T(8,128)}, f32[128,128]{1,0:T(8,128)}) custom-call(s32[8,8,512]{2,1,0:T(8,128)} %fusion.2.code_ref, bf16[512,128]{1,0:T(8,128)(2,1)} %grads_ref.1, f32[4096,128]{1,0:T(8,128)} %table_ref.1, f32[32,128]{1,0:T(8,128)} %bitcast.10, s32[32,128]{1,0:T(8,128)} %bitcast.11), custom_call_target="tpu_custom_call" | custom-call | tf_op jit(solution)/shard_map/step/pallas_call | solution.py:470
  87.8 3.8 %publish.1 = (bf16[512,128]{1,0:T(8,128)(2,1)}, f32[4096,128]{1,0:T(8,128)}, f32[32,128]{1,0:T(8,128)}, f32[128,128]{1,0:T(8,128)}) custom-call(bf16[512,128]{1,0:T(8,128)(2,1)} %get-tuple-element.12.pooled, f32[4096,128]{1,0:T(8,128)} %get-tuple-element.13.fresh, f32[32,128]{1,0:T(8,128)} %get-tuple-element.14.accum, f32[128,128]{1,0:T(8,128)} %get-tuple-element.15.change, ...), custom_call_target="tpu_custom_call" | custom-call | tf_op jit(solution)/shard_map/publish/pallas_call | solution.py:537
  (1 shorter events, 0.0 us)

commit v6 on v5

--- a/solution.py
+++ b/solution.py
@@ -456,11 +456,11 @@
     index = jnp.arange(table_count, dtype=I32)
     owner_at = (index % NQ // NC * NZ + index // NQ) * NC + index % NC
     named = owners.T[:, None, :] == owner_at[None, :, None]
-    hits = jnp.any(named, axis=0)
-    wanted = jnp.sum(jnp.where(named, local_rows.T[:, None, :], 0), axis=0)
+    wanted = jnp.sum(jnp.where(named, local_rows.T[:, None, :] + 1, 0), axis=0)
+    hits = wanted > 0
     before = jnp.arange(bags)[:, None] < jnp.arange(bags)[None, :]
     rank = jnp.dot(hits.astype(BF16), before.astype(BF16), preferred_element_type=F32)
-    code = jnp.where(hits, wanted * CAP + rank.astype(I32), -1).reshape(NZ, NQ, bags)
+    code = jnp.where(hits, (wanted - 1) * CAP + rank.astype(I32), -1).reshape(NZ, NQ, bags)
 
     count = parity.shape[0]
     share = count // dp

time: 92.6 us -> 92.3 us (level)
  no operation moved by 1% of the time
where the time goes in v6:
time: 92.3 us; the launch traced here: 91.6 us
  Pallas kernels  88.3 us (96%)
  other arithmetic  1.63 us (2%)
    pallas_call x1, Pallas kernels, on_device(): pl.pallas_call(step_kernel, out_shape=(jax.ShapeDtypeStruct((bags, width)...  84.5 us
    pallas_call x1, Pallas kernels, on_device(): pl.pallas_call(publish_kernel, grid=(4,), out_shape=tuple((jax.ShapeDtype...  3.82 us

profile of v6, /device:TPU:32, one launch (start us, length us, event | category | flops | bytes accessed | tf_op | source)
XLA Modules:
  0.0 91.6 jit_solution(10539847958289608919)
XLA Ops:
  0.6 0.7 add_bitcast_fusion
  1.4 0.9 select_reduce_fusion
  2.3 0.9 fusion.2.code_ref
  3.1 84.5 %step.1 = (bf16[512,128]{1,0:T(8,128)(2,1)}, f32[4096,128]{1,0:T(8,128)}, f32[32,128]{1,0:T(8,128)}, f32[128,128]{1,0:T(8,128)}) custom-call(s32[8,8,512]{2,1,0:T(8,128)} %fusion.2.code_ref, bf16[512,128]{1,0:T(8,128)(2,1)} %grads_ref.1, f32[4096,128]{1,0:T(8,128)} %table_ref.1, f32[32,128]{1,0:T(8,128)} %bitcast.8, s32[32,128]{1,0:T(8,128)} %bitcast.9), custom_call_target="tpu_custom_call" | custom-call | tf_op jit(solution)/shard_map/step/pallas_call | solution.py:470
  87.6 3.8 %publish.1 = (bf16[512,128]{1,0:T(8,128)(2,1)}, f32[4096,128]{1,0:T(8,128)}, f32[32,128]{1,0:T(8,128)}, f32[128,128]{1,0:T(8,128)}) custom-call(bf16[512,128]{1,0:T(8,128)(2,1)} %get-tuple-element.12.pooled, f32[4096,128]{1,0:T(8,128)} %get-tuple-element.13.fresh, f32[32,128]{1,0:T(8,128)} %get-tuple-element.14.accum, f32[128,128]{1,0:T(8,128)} %get-tuple-element.15.change, ...), custom_call_target="tpu_custom_call" | custom-call | tf_op jit(solution)/shard_map/publish/pallas_call | solution.py:537
  (1 shorter events, 0.0 us)
